TPU v7x, 32 devices: a whole 2x2x4 slice. The times are simulated.
32 devices in a mesh: member: 2 (over core), fsdp: 16 (over z, y, x).
Axes of the slice: x: 2, y: 2, z: 4, core: 2. Of those that a mesh axis runs over, the one named last changes fastest.
Arguments:
- hidden: bfloat16 [2, 512, 2048], P('member', 'fsdp'), may hold values from -60 to 60
- gain: float32 [2, 2048], P('member'), may hold values from 0.5 to 1.5
- head: bfloat16 [2, 2048, 128256], P('member', None, 'fsdp'), may hold values from -0.397747564 to 0.397747564
- labels: int32 [512], replicated, may hold values from 0 to 128255
Outputs:
- token_loss: float32 [2, 512], P('member', 'fsdp')
- head_grad: bfloat16 [2, 2048, 128256], P('member', None, 'fsdp')
- hidden_grad: bfloat16 [2, 512, 2048], P('member', 'fsdp')
All inputs are finite; a program needn't handle non-finite values.
Results may differ from a plain program's by a relative error of at most 0.0049.
Values may be sent and summed in bfloat16 or wider, within the bound.
No kernel may reach another device: no remote copies, remote signals or barrier semaphores. Data moves between devices by JAX's collectives and lax.ppermute only.
A program may use at most 128 MiB of HBM per device.

v0:
```python
import jax
import jax.numpy as jnp
from jax import lax
from jax.sharding import PartitionSpec as P

EPS = 1e-05
BETA = 0.5


def swapped(value, axis, bit):
    return lax.ppermute(value, axis, [(i, i ^ 1 << bit) for i in range(lax.axis_size(axis))])


def normalize(rows, gain_row):
    values = rows.astype(jnp.float32)
    inverse = lax.rsqrt(jnp.mean(values * values, axis=-1, keepdims=True) + EPS)
    return ((values * inverse * gain_row).astype(jnp.bfloat16), inverse)


def norm_back(rows, inverse, gain_row, upstream):
    values = rows.astype(jnp.float32)
    scaled = gain_row * upstream
    inner = jnp.mean(scaled * values, axis=-1, keepdims=True)
    return inverse * scaled - values * inverse**3 * inner


def body(hidden, gain, head, labels):
    own_rows = hidden[0]
    gain_row = gain[0]
    weights_local = head[0]
    tok_dev = own_rows.shape[0]
    vocab_dev = weights_local.shape[1]
    own_start = lax.axis_index("fsdp") * tok_dev
    vocab_start = lax.axis_index("fsdp") * vocab_dev
    normed_own, inverse_own = normalize(own_rows, gain_row)
    normed = lax.all_gather(normed_own, "fsdp", axis=0, tiled=True)
    token_count = normed.shape[0]
    logits = jnp.dot(normed, weights_local, preferred_element_type=jnp.float32)
    local_label = labels - vocab_start
    columns = lax.broadcasted_iota(jnp.int32, (1, vocab_dev), 1)
    onehot_mask = local_label[:, None] == columns
    picked_part = jnp.sum(jnp.where(onehot_mask, logits, 0.0), axis=-1)
    row_top = lax.pmax(jnp.max(logits, axis=-1), "fsdp")
    row_total, picked = lax.psum(
        (jnp.sum(jnp.exp(logits - row_top[:, None]), axis=-1), picked_part), "fsdp"
    )
    log_total = row_top + jnp.log(row_total)
    logprob = (logits - log_total[:, None]).astype(jnp.bfloat16)
    teacher = swapped(logprob, "member", 0)
    target = jnp.exp(teacher.astype(jnp.float32))
    student = jnp.exp(logits - log_total[:, None])
    dlogits = (
        ((1.0 + BETA) * student - onehot_mask.astype(jnp.float32) - BETA * target) / token_count
    ).astype(jnp.bfloat16)
    cross_part = jnp.sum(target * (log_total[:, None] - logits), axis=-1)
    head_grad = lax.dot_general(
        normed, dlogits, (((0,), (0,)), ((), ())), preferred_element_type=jnp.float32
    ).astype(jnp.bfloat16)
    cross_whole = lax.psum(cross_part, "fsdp")
    cross_own = lax.dynamic_slice_in_dim(cross_whole, own_start, tok_dev, 0)
    partial_up = lax.dot_general(
        dlogits, weights_local, (((1,), (1,)), ((), ())), preferred_element_type=jnp.float32
    )
    summed = lax.psum_scatter(partial_up, "fsdp", scatter_dimension=0, tiled=True)
    total_own = lax.dynamic_slice_in_dim(log_total, own_start, tok_dev, 0)
    picked_own = lax.dynamic_slice_in_dim(picked, own_start, tok_dev, 0)
    token_loss = total_own - picked_own + BETA * cross_own
    hidden_grad = norm_back(own_rows, inverse_own, gain_row, summed)
    return (token_loss[None], head_grad[None], hidden_grad.astype(jnp.bfloat16)[None])


def solution(mesh):
    in_specs = (P("member", "fsdp", None), P("member", None), P("member", None, "fsdp"), P())
    out_specs = (P("member", "fsdp"), P("member", None, "fsdp"), P("member", "fsdp", None))
    return jax.shard_map(body, mesh=mesh, in_specs=in_specs, out_specs=out_specs, check_vma=False)
```

profile of v0, /device:TPU:0, one launch (start us, length us, event | category | flops | bytes accessed | tf_op | source)
XLA Modules:
  0.0 349.3 jit_solution(791102755246308819)
XLA Ops:
  7.2 0.0 all-gather.2.cloned.1.call-start
  7.2 1.0 fusion.4
  8.3 1.7 fusion.6
  9.9 0.0 all-gather.2.cloned.1.call-update
  10.0 0.0 reduce-scatter.2.cloned.1.call-start
  10.0 64.8 %all-gather.2.cloned.1.call-done = bf16[512,2048]{1,0:T(8,128)(2,1)} async-done(((bf16[32,2048]{1,0:T(8,128)(2,1)}), bf16[512,2048]{1,0:T(8,128)(2,1)}) %all-gather.2.cloned.1.call-update) | async-done | bytes 2097168 | tf_op jit(solution)/shard_map/all_gather | solution.py:36
  74.8 25.0 %fusion.12 = (f32[512]{0:T(512)S(1)}, f32[512,8016]{0,1:T(8,128)}) fusion(bf16[512,2048]{1,0:T(8,128)(2,1)} %all-gather.2.cloned.1.call-done, bf16[1,2048,8016]{1,2,0:T(8,128)(2,1)} %param.6), kind=kOutput, calls=%fused_computation.30 | convolution fusion | flops 16814874624 | bytes 51349504 | tf_op jit(solution)/shard_map/dot_general | solution.py:38
  99.8 39.4 %pmax.7 = f32[512]{0:T(512)S(1)} all-reduce(f32[512]{0:T(512)S(1)} %get-tuple-element.10), channel_id=1, replica_groups=mesh['member'=2,'fsdp'=16] {'fsdp'}, use_global_device_ids=true, to_apply=%region_2.3 | all-reduce | flops 512 | bytes 4096 | tf_op jit(solution)/shard_map/pmax | solution.py:43
  139.2 7.9 %exponential_reduce_fusion = f32[512]{0:T(512)S(1)} fusion(f32[512,8016]{0,1:T(8,128)} %get-tuple-element.11, f32[512]{0:T(512)S(1)} %pmax.7), kind=kLoop, calls=%fused_computation.10 | loop fusion | flops 8207872 | bytes 16420864 | tf_op jit(solution)/shard_map/reduce_sum | solution.py:45
  147.1 36.7 %psum.21 = f32[512]{0:T(512)S(1)} all-reduce(f32[512]{0:T(512)S(1)} %exponential_reduce_fusion), channel_id=1, replica_groups=mesh['member'=2,'fsdp'=16] {'fsdp'}, use_global_device_ids=true, to_apply=%region_4.5 | all-reduce | flops 512 | bytes 4096 | tf_op jit(solution)/shard_map/psum | solution.py:44
  183.8 8.8 %subtract_convert_fusion = bf16[512,8016]{0,1:T(8,128)(2,1)} fusion(f32[512,8016]{0,1:T(8,128)} %get-tuple-element.11, f32[512]{0:T(512)S(1)} %log_add_fusion), kind=kLoop, calls=%fused_computation.11 | loop fusion | flops 8208384 | bytes 24627200 | tf_op jit(solution)/shard_map/convert_element_type | solution.py:48
  192.7 0.0 collective-permute-start
  192.7 0.0 copy-done.3
  192.7 13.2 %collective-permute-done = bf16[512,8016]{0,1:T(8,128)(2,1)} collective-permute-done((bf16[512,8016]{0,1:T(8,128)(2,1)}, bf16[512,8016]{0,1:T(8,128)(2,1)}, u32[]{:S(2)}, u32[]{:S(2)}) %collective-permute-start) | collective-permute-done | bytes 8208416 | tf_op jit(solution)/shard_map/ppermute | solution.py:11
  205.9 13.7 %select_reduce_fusion = (f32[512]{0:T(512)S(1)}, f32[512]{0:T(512)S(1)}, bf16[512,8016]{0,1:T(8,128)(2,1)S(1)}) fusion(f32[512,8016]{0,1:T(8,128)} %get-tuple-element.11, s32[512]{0:T(512)S(1)} %broadcast_subtract_fusion, f32[512]{0:T(512)S(1)} %log_add_fusion, bf16[512,8016]{0,1:T(8,128)(2,1)} %collective-permute-done), kind=kLoop, calls=%fused_computation.8 | loop fusion | flops 61561856 | bytes 32841728 | tf_op jit(solution)/shard_map/reduce_sum | solution.py:42
  219.6 3.1 copy-done
  222.8 22.6 %fusion = f32[512,2048]{1,0:T(8,128)} fusion(bf16[512,8016]{0,1:T(8,128)(2,1)S(1)} %get-tuple-element.7, bf16[1,2048,8016]{1,2,0:T(8,128)(2,1)} %param.6), kind=kOutput, calls=%fused_computation | convolution fusion | flops 16810770432 | bytes 45236224 | tf_op jit(solution)/shard_map/dot_general | solution.py:61
  245.4 0.0 reduce-scatter.2.cloned.1.call-update
  245.4 39.0 %all-reduce = (f32[512]{0:T(512)S(1)}, f32[512]{0:T(512)S(1)}) all-reduce(f32[512]{0:T(512)S(1)} %get-tuple-element.4, f32[512]{0:T(512)S(1)} %get-tuple-element.3), channel_id=1, replica_groups=mesh['member'=2,'fsdp'=16] {'fsdp'}, use_global_device_ids=true, to_apply=%region_8.9 | all-reduce | flops 1024 | bytes 8192 | tf_op jit(solution)/shard_map/psum | solution.py:59
  284.4 0.6 add_bitcast_fusion
  285.0 24.5 %convert_bitcast_fusion = bf16[1,2048,8016]{1,2,0:T(8,128)(2,1)} fusion(bf16[512,8016]{0,1:T(8,128)(2,1)} %copy-done, bf16[512,2048]{1,0:T(8,128)(2,1)S(1)} %copy-done.4), kind=kOutput, calls=%fused_computation.4 | convolution fusion | flops 16827187200 | bytes 43139072 | tf_op jit(solution)/shard_map/dot_general | solution.py:56
  309.6 30.1 %reduce-scatter.2.cloned.1.call-done = f32[32,2048]{1,0:T(8,128)} async-done(((f32[512,2048]{1,0:T(8,128)}), f32[32,2048]{1,0:T(8,128)}) %reduce-scatter.2.cloned.1.call-update) | async-done | bytes 262160 | tf_op jit(solution)/shard_map/reduce_scatter | solution.py:64
  339.6 1.1 fusion.10
  340.7 1.7 fusion.11
  (12 shorter events, 0.0 us)
Async XLA Ops:
  7.2 67.6 %all-gather.2.cloned.1.call-start = ((), (), s32[]{:S(2)}) async-start(), calls=%async_computation.1 | async-start | bytes 2228224 | tf_op jit(solution)/shard_map/all_gather | solution.py:36
  10.0 329.7 %reduce-scatter.2.cloned.1.call-start = ((), (), s32[]{:S(2)}) async-start(), calls=%async_computation.2 | async-start | bytes 4456448 | tf_op jit(solution)/shard_map/reduce_scatter | solution.py:64
  147.1 45.6 %copy-start.3 = (s32[512]{0:T(512)S(1)}, s32[512]{0:T(512)}, u32[]{:S(2)}) copy-start(s32[512]{0:T(512)} %param.7) | copy-start | bytes 6148
  192.7 13.2 %collective-permute-start = (bf16[512,8016]{0,1:T(8,128)(2,1)}, bf16[512,8016]{0,1:T(8,128)(2,1)}, u32[]{:S(2)}, u32[]{:S(2)}) collective-permute-start(bf16[512,8016]{0,1:T(8,128)(2,1)} %subtract_convert_fusion), channel_id=1, source_target_pairs={{0,16},{16,0},{1,17},{17,1},{2,18},{18,2},{3,19},{19,3},{4,20},{20... | collective-permute-start | bytes 24625160 | tf_op jit(solution)/shard_map/ppermute | solution.py:11
  219.6 3.2 copy-start
  222.8 62.3 %copy-start.4 = (bf16[512,2048]{1,0:T(8,128)(2,1)S(1)}, bf16[512,2048]{1,0:T(8,128)(2,1)}, u32[]{:S(2)}) copy-start(bf16[512,2048]{1,0:T(8,128)(2,1)} %all-gather.2.cloned.1.call-done) | copy-start | bytes 6291460
  285.0 54.6 %copy-start.1 = (bf16[1,32,2048]{2,1,0:T(8,128)(2,1)S(1)}, bf16[1,32,2048]{2,1,0:T(8,128)(2,1)}, u32[]{:S(2)}) copy-start(bf16[1,32,2048]{2,1,0:T(8,128)(2,1)} %param.4) | copy-start | bytes 393220
  285.0 54.6 %copy-start.2 = (f32[1,2048]{1,0:T(1,128)S(1)}, f32[1,2048]{1,0:T(1,128)}, u32[]{:S(2)}) copy-start(f32[1,2048]{1,0:T(1,128)} %param.5) | copy-start | bytes 24580
Sparse Core Ops, SparseCore 0:
  11.3 63.3 all-gather.1
  245.5 94.0 reduce-scatter.1
where the time goes:
time: 350 us; the launch traced here: 349 us
  blocking collectives  115 us (33%)
  waiting for transfers between devices  108 us (31%)
  matrix products  72.1 us (21%)
  other arithmetic  36.5 us (10%)
  between operations  14.1 us (4%)
    all_gather x1, waiting for transfers between devices, body(): normed = lax.all_gather(normed_own, 'fsdp', axis=0, tiled=True)  64.8 us
    pmax x1, blocking collectives, body(): row_top = lax.pmax(jnp.max(logits, axis=-1), 'fsdp')  39.4 us
    psum x1, blocking collectives, body(): cross_whole = lax.psum(cross_part, 'fsdp')  39 us
    psum x1, blocking collectives, body(): lax.psum((jnp.sum(jnp.exp(logits - row_top[:, None]), axis=-1), picked_pa...  36.7 us
    reduce_scatter x1, waiting for transfers between devices, body(): lax.psum_scatter(partial_up, 'fsdp', scatter_dimension=0, tiled=True)  30.1 us
    dot_general x1, matrix products, body(): logits = jnp.dot(normed, weights_local, preferred_element_type=jnp.float32)  25 us
    dot_general x1, matrix products, body(): lax.dot_general(normed, dlogits, (((0,), (0,)), ((), ())), preferred_elem...  24.5 us
    dot_general x1, matrix products, body(): lax.dot_general(dlogits, weights_local, (((1,), (1,)), ((), ())), preferr...  22.6 us
  transfers between devices with their start and end apart: 3, of which 3 were waited for; matrix products, arithmetic and copies ran while one was open for 7% of the time, Pallas kernels for 0%

commit v1 on v0

v1 whole, which is shorter than its diff:
```python
import functools
import jax
import jax.numpy as jnp
from jax import lax
from jax.experimental import pallas as pl
from jax.experimental.pallas import tpu as pltpu
from jax.sharding import PartitionSpec as P

EPS = 1e-05
BETA = 0.5
TILE = 1024
CHUNK = 128
LANES = 128
VMEM_LIMIT = 56 * 1024 * 1024


def cdiv(a, b):
    return -(-a // b)


def flip_bit(value, axis_name, bit):
    n = lax.axis_size(axis_name)
    return lax.ppermute(value, axis_name, [(i, i ^ (1 << bit)) for i in range(n)])


def tiling(vocab_dev):
    tile = min(TILE, cdiv(vocab_dev, 16) * 16)
    return tile, cdiv(vocab_dev, tile)


def whole(shape):
    return pl.BlockSpec(shape, lambda j: (0, 0))


def chunks(valid):
    return [
        (start, min(CHUNK, cdiv(valid - start, 16) * 16), min(CHUNK, valid - start))
        for start in range(0, valid, CHUNK)
    ]


def pick_row(table, index):
    here = lax.broadcasted_iota(jnp.int32, table.shape, 0) == index
    return jnp.sum(jnp.where(here, table, 0.0), axis=0, keepdims=True)


def logits_kernel(
    vocab_dev, tile, tiles, hidden_ref, gain_ref, labels_ref, w_ref,
    p_ref, l_ref, normed_ref, m_ref, stats_ref, logits_ref, s_ref, picked_ref,
):
    step = pl.program_id(0)
    tokens = hidden_ref.shape[0]

    def matmul(slot):
        logits_ref[slot] = lax.dot_general(
            w_ref[...], normed_ref[...], (((1,), (1,)), ((), ())), preferred_element_type=jnp.float32
        )

    def soften(slot, index, valid_rows):
        group = min(tokens, LANES)
        for col in range(0, tokens, group):
            cols = slice(col, col + group)
            target = labels_ref[:, cols] - index * tile
            top = None
            for start, rows, valid in chunks(valid_rows):
                values = logits_ref[slot, start : start + valid, cols]
                part = jnp.max(values, axis=0, keepdims=True)
                top = part if top is None else jnp.maximum(top, part)
            total = jnp.zeros((1, group), jnp.float32)
            picked = picked_ref[:, cols]
            for start, rows, valid in chunks(valid_rows):
                values = logits_ref[slot, start : start + rows, cols]
                row = lax.broadcasted_iota(jnp.int32, (rows, group), 0)
                lowered = values - top
                exps = jnp.exp(lowered)
                l_ref[start : start + rows, cols] = lowered.astype(l_ref.dtype)
                p_ref[start : start + rows, cols] = exps.astype(p_ref.dtype)
                chosen = jnp.where(row == target - start, values, 0.0)
                if valid < rows:
                    exps = jnp.where(row < valid, exps, 0.0)
                    chosen = jnp.where(row < valid, chosen, 0.0)
                total = total + jnp.sum(exps, axis=0, keepdims=True)
                picked = picked + jnp.sum(chosen, axis=0, keepdims=True)
            here = lax.broadcasted_iota(jnp.int32, (m_ref.shape[0], group), 0) == index
            m_ref[:, cols] = jnp.where(here, top, m_ref[:, cols])
            s_ref[:, cols] = jnp.where(here, total, s_ref[:, cols])
            picked_ref[:, cols] = picked

    @pl.when(step == 0)
    def _():
        for row in range(0, tokens, CHUNK):
            rows = slice(row, row + CHUNK)
            values = hidden_ref[rows, :].astype(jnp.float32)
            inverse = lax.rsqrt(jnp.mean(values * values, axis=-1, keepdims=True) + EPS)
            normed_ref[rows, :] = (values * inverse * gain_ref[...]).astype(jnp.bfloat16)
        m_ref[...] = jnp.full_like(m_ref, -jnp.inf)
        s_ref[...] = jnp.zeros_like(s_ref)
        picked_ref[...] = jnp.zeros_like(picked_ref)
        matmul(0)

    if tiles > 1:

        @pl.when((step > 0) & (step < tiles))
        def _():
            matmul(lax.rem(step, 2))
            soften(lax.rem(step + 1, 2), step - 1, tile)

    @pl.when(step == tiles)
    def _():
        soften((tiles - 1) % 2, tiles - 1, vocab_dev - (tiles - 1) * tile)
        tops = m_ref[...]
        top = jnp.max(tops, axis=0, keepdims=True)
        total = jnp.sum(s_ref[...] * jnp.exp(tops - top), axis=0, keepdims=True)
        stats_ref[...] = jnp.zeros_like(stats_ref)
        stats_ref[0:1, :] = top
        stats_ref[1:2, :] = total
        stats_ref[2:3, :] = picked_ref[...]


def run_logits(hidden, gain, labels, weights):
    tokens, width = hidden.shape
    vocab_dev = weights.shape[0]
    tile, tiles = tiling(vocab_dev)
    groups = cdiv(tiles, 8) * 8
    behind = pl.BlockSpec((tile, tokens), lambda j: (jnp.maximum(j - 1, 0), 0))
    return pl.pallas_call(
        functools.partial(logits_kernel, vocab_dev, tile, tiles),
        grid=(tiles + 1,),
        in_specs=[
            whole((tokens, width)),
            whole((1, width)),
            whole((1, tokens)),
            pl.BlockSpec((tile, width), lambda j: (jnp.minimum(j, tiles - 1), 0)),
        ],
        out_specs=[behind, behind, whole((tokens, width)), whole((groups, tokens)), whole((8, tokens))],
        out_shape=[
            jax.ShapeDtypeStruct((vocab_dev, tokens), jnp.bfloat16),
            jax.ShapeDtypeStruct((vocab_dev, tokens), jnp.bfloat16),
            jax.ShapeDtypeStruct((tokens, width), jnp.bfloat16),
            jax.ShapeDtypeStruct((groups, tokens), jnp.float32),
            jax.ShapeDtypeStruct((8, tokens), jnp.float32),
        ],
        scratch_shapes=[
            pltpu.VMEM((2, tile, tokens), jnp.float32),
            pltpu.VMEM((groups, tokens), jnp.float32),
            pltpu.VMEM((1, tokens), jnp.float32),
        ],
        compiler_params=pltpu.CompilerParams(vmem_limit_bytes=VMEM_LIMIT),
        cost_estimate=pl.CostEstimate(
            flops=2 * tokens * width * vocab_dev,
            bytes_accessed=2 * width * vocab_dev + 4 * tokens * vocab_dev,
            transcendentals=tokens * vocab_dev,
        ),
        name="logits",
    )(hidden, gain, labels, weights)


def dlogits_kernel(
    vocab_dev, tile, tiles, totals_ref, labels_ref, ms_ref, mt_ref, ps_ref, pt_ref, l_ref, w_ref,
    d_ref, up_ref, cross_ref, d_scratch, a_ref, b_ref, g_ref, c_ref,
):
    step = pl.program_id(0)
    tokens = ps_ref.shape[1]
    scale = 1.0 / tokens
    last_rows = vocab_dev - (tiles - 1) * tile

    def weigh(slot, index, valid_rows):
        group = min(tokens, LANES)
        for col in range(0, tokens, group):
            cols = slice(col, col + group)
            target = labels_ref[:, cols] - index * tile
            own, other, gap = (pick_row(ref[:, cols], index) for ref in (a_ref, b_ref, g_ref))
            cross = c_ref[:, cols]
            for start, rows, valid in chunks(valid_rows):
                here = slice(start, start + rows)
                row = lax.broadcasted_iota(jnp.int32, (rows, group), 0)
                student = ps_ref[here, cols].astype(jnp.float32) * own
                teacher = pt_ref[here, cols].astype(jnp.float32) * other
                lowered = l_ref[here, cols].astype(jnp.float32)
                part = teacher * (gap - lowered)
                value = student - teacher - jnp.where(row == target - start, scale, 0.0)
                if valid < rows:
                    part = jnp.where(row < valid, part, 0.0)
                    value = jnp.where(row < valid, value, 0.0)
                cross = cross + jnp.sum(part, axis=0, keepdims=True)
                value = value.astype(jnp.bfloat16)
                d_ref[here, cols] = value
                d_scratch[slot, here, cols] = value
            c_ref[:, cols] = cross

    def matmul(slot, valid_rows):
        depth = cdiv(valid_rows, 16) * 16
        if valid_rows % 16:
            edge = slice(depth - 16, depth)
            row = lax.broadcasted_iota(jnp.int32, (16, w_ref.shape[1]), 0)
            w_ref[edge, :] = jnp.where(row < valid_rows - depth + 16, w_ref[edge, :], jnp.zeros((), w_ref.dtype))
        for start in range(0, up_ref.shape[1], 512):
            out = slice(start, start + 512)
            up_ref[:, out] += lax.dot_general(
                d_scratch[slot, :depth, :], w_ref[:depth, out], (((0,), (0,)), ((), ())),
                preferred_element_type=jnp.float32,
            )

    @pl.when(step == 0)
    def _():
        own_total, other_total = totals_ref[0:1, :], totals_ref[1:2, :]
        a_ref[...] = jnp.exp(ms_ref[...] - own_total) * ((1.0 + BETA) * scale)
        b_ref[...] = jnp.exp(mt_ref[...] - other_total) * (BETA * scale)
        g_ref[...] = own_total - ms_ref[...]
        c_ref[...] = jnp.zeros_like(c_ref)
        up_ref[...] = jnp.zeros_like(up_ref)
        weigh(0, 0, last_rows if tiles == 1 else tile)

    if tiles > 2:

        @pl.when((step > 0) & (step < tiles - 1))
        def _():
            matmul(lax.rem(step + 1, 2), tile)
            weigh(lax.rem(step, 2), step, tile)

    if tiles > 1:

        @pl.when(step == tiles - 1)
        def _():
            matmul(tiles % 2, tile)
            weigh((tiles - 1) % 2, tiles - 1, last_rows)

    @pl.when(step == tiles)
    def _():
        matmul((tiles - 1) % 2, last_rows)
        cross_ref[...] = jnp.broadcast_to(c_ref[...] * (tokens / BETA), cross_ref.shape)


def run_dlogits(totals, labels, m_own, m_other, p_own, p_other, lowered, weights):
    tokens = p_own.shape[1]
    vocab_dev, width = weights.shape
    tile, tiles = tiling(vocab_dev)
    groups = m_own.shape[0]
    here = pl.BlockSpec((tile, tokens), lambda j: (jnp.minimum(j, tiles - 1), 0))
    return pl.pallas_call(
        functools.partial(dlogits_kernel, vocab_dev, tile, tiles),
        grid=(tiles + 1,),
        in_specs=[
            whole((8, tokens)),
            whole((1, tokens)),
            whole((groups, tokens)),
            whole((groups, tokens)),
            here,
            here,
            here,
            pl.BlockSpec((tile, width), lambda j: (jnp.maximum(j - 1, 0), 0)),
        ],
        out_specs=[here, whole((tokens, width)), whole((8, tokens))],
        out_shape=[
            jax.ShapeDtypeStruct((vocab_dev, tokens), jnp.bfloat16),
            jax.ShapeDtypeStruct((tokens, width), jnp.float32),
            jax.ShapeDtypeStruct((8, tokens), jnp.float32),
        ],
        scratch_shapes=[
            pltpu.VMEM((2, tile, tokens), jnp.bfloat16),
            pltpu.VMEM((groups, tokens), jnp.float32),
            pltpu.VMEM((groups, tokens), jnp.float32),
            pltpu.VMEM((groups, tokens), jnp.float32),
            pltpu.VMEM((1, tokens), jnp.float32),
        ],
        compiler_params=pltpu.CompilerParams(vmem_limit_bytes=VMEM_LIMIT),
        cost_estimate=pl.CostEstimate(
            flops=2 * tokens * width * vocab_dev,
            bytes_accessed=2 * width * vocab_dev + 8 * tokens * vocab_dev,
            transcendentals=0,
        ),
        name="dlogits",
    )(totals, labels, m_own, m_other, p_own, p_other, lowered, weights)


def head_grad_kernel(normed_ref, d_ref, out_ref):
    out_ref[...] = jnp.dot(d_ref[...], normed_ref[...], preferred_element_type=jnp.float32).astype(out_ref.dtype)


def run_head_grad(normed, dlogits):
    tokens, width = normed.shape
    vocab_dev = dlogits.shape[0]
    tile, tiles = tiling(vocab_dev)
    return pl.pallas_call(
        head_grad_kernel,
        grid=(tiles,),
        in_specs=[whole((tokens, width)), pl.BlockSpec((tile, tokens), lambda j: (j, 0))],
        out_specs=pl.BlockSpec((tile, width), lambda j: (j, 0)),
        out_shape=jax.ShapeDtypeStruct((vocab_dev, width), jnp.bfloat16),
        compiler_params=pltpu.CompilerParams(vmem_limit_bytes=VMEM_LIMIT),
        cost_estimate=pl.CostEstimate(
            flops=2 * tokens * width * vocab_dev,
            bytes_accessed=2 * width * vocab_dev + 2 * tokens * vocab_dev,
            transcendentals=0,
        ),
        name="head_grad",
    )(normed, dlogits)


def gather_blocks(own, bits):
    held = own[None]
    for bit in reversed(range(bits)):
        arrived = flip_bit(held, "fsdp", bit)
        held = jnp.stack([held, arrived])
        held = held.reshape((-1,) + own.shape)
    return held


def place_bits(bits):
    offsets = [0]
    for bit in reversed(range(bits)):
        offsets = offsets + [o | 1 << bit for o in offsets]
    return offsets


def swap_halves(value, axis):
    low, high = jnp.split(value, 2, axis=axis)
    return jnp.concatenate([high, low], axis=axis)


def merge(own, other):
    top = jnp.maximum(own[0::3], other[0::3])
    total = own[1::3] * jnp.exp(own[0::3] - top) + other[1::3] * jnp.exp(other[0::3] - top)
    picked = own[2::3] + other[2::3]
    parts = []
    for i in range(top.shape[0]):
        parts += [top[i : i + 1], total[i : i + 1], picked[i : i + 1]]
    return jnp.concatenate(parts, axis=0)


def body(hidden, gain, head, labels):
    own_rows = hidden[0]
    gain_row = gain[0]
    weights = head[0].T
    tok_dev, width = own_rows.shape
    vocab_dev = weights.shape[0]
    count = lax.axis_size("fsdp")
    bits = count.bit_length() - 1
    index = lax.axis_index("fsdp")
    tokens = tok_dev * count

    rows = gather_blocks(own_rows, bits).reshape(tokens, width)
    offsets = jnp.asarray(place_bits(bits), jnp.int32)
    local_labels = (
        labels.reshape(count, tok_dev)[offsets ^ index].reshape(1, tokens) - index * vocab_dev
    )

    p_own, lowered, normed, m_own, stats = run_logits(rows, gain_row[None], local_labels, weights)

    p_other = flip_bit(p_own, "member", 0)
    m_other = flip_bit(m_own, "member", 0)

    table = stats[:3]
    for bit in range(bits):
        arrived = flip_bit(table, "fsdp", bit)
        place = bits - 1 - bit
        block = tok_dev << place
        arrived = swap_halves(arrived.reshape(3, tokens // (2 * block), 2 * block), 2).reshape(3, tokens)
        table = merge(table, arrived)
    log_total = table[0] + jnp.log(table[1])
    picked = table[2]
    other_total = flip_bit(log_total, "member", 0)
    totals = jnp.concatenate([log_total[None], other_total[None], jnp.zeros((6, tokens), jnp.float32)])

    dlogits, partial_up, cross = run_dlogits(
        totals, local_labels, m_own, m_other, p_own, p_other, lowered, weights
    )

    summed = partial_up
    cross_sum = cross[0]
    for bit in range(bits):
        half = summed.shape[0] // 2
        arrived = flip_bit(summed[half:].astype(jnp.bfloat16), "fsdp", bit)
        summed = summed[:half] + arrived.astype(jnp.float32)
        arrived = flip_bit(cross_sum[half:], "fsdp", bit)
        cross_sum = cross_sum[:half] + arrived

    head_grad = run_head_grad(normed, dlogits).T

    token_loss = log_total[:tok_dev] - picked[:tok_dev] + BETA * cross_sum
    values = own_rows.astype(jnp.float32)
    inverse = lax.rsqrt(jnp.mean(values * values, axis=-1, keepdims=True) + EPS)
    scaled = gain_row * summed
    inner = jnp.mean(scaled * values, axis=-1, keepdims=True)
    hidden_grad = inverse * scaled - values * inverse**3 * inner
    return (token_loss[None], head_grad[None], hidden_grad.astype(jnp.bfloat16)[None])


def solution(mesh):
    in_specs = (P("member", "fsdp", None), P("member", None), P("member", None, "fsdp"), P())
    out_specs = (P("member", "fsdp"), P("member", None, "fsdp"), P("member", "fsdp", None))
    return jax.shard_map(body, mesh=mesh, in_specs=in_specs, out_specs=out_specs, check_vma=False)
```

time: 350 us -> 223 us (0.64)
  blocking collectives: 115 us -> 0 us
  Pallas kernels: 0 us -> 86.9 us
  matrix products: 72.1 us -> 0 us
  starting transfers between devices: 0.08 us -> 29.2 us
  other arithmetic: 36.5 us -> 8 us
  waiting for transfers between devices: 108 us -> 91.4 us
  between operations: 14.1 us -> 0.88 us
    pallas_call x0 -> x3, Pallas kernels: none -> 86.9 us  [the longest x1 32.5 us: run_dlogits(): pl.pallas_call(functools.partial(dlogits_kernel, vocab_dev, tile, tiles),...]
    ppermute x1 -> x19, waiting for transfers between devices: 13.2 us -> 91.4 us  [flip_bit(): return lax.ppermute(value, axis_name, [(i, i ^ 1 << bit) for i in range(n)])]
    psum x2 -> x0, blocking collectives: 75.8 us -> none  [the longest x1 39 us: body(): cross_whole = lax.psum(cross_part, 'fsdp')]
    dot_general x3 -> x0, matrix products: 72.1 us -> none  [the longest x1 25 us: body(): logits = jnp.dot(normed, weights_local, preferred_element_type=jnp.float32)]
    all_gather x1 -> x0, waiting for transfers between devices: 64.8 us -> none  [body(): normed = lax.all_gather(normed_own, 'fsdp', axis=0, tiled=True)]
    pmax x1 -> x0, blocking collectives: 39.4 us -> none  [body(): row_top = lax.pmax(jnp.max(logits, axis=-1), 'fsdp')]
    reduce_scatter x1 -> x0, waiting for transfers between devices: 30.1 us -> none  [body(): lax.psum_scatter(partial_up, 'fsdp', scatter_dimension=0, tiled=True)]
    ppermute x1 -> x19, starting transfers between devices: 0.01 us -> 29.2 us  [flip_bit(): return lax.ppermute(value, axis_name, [(i, i ^ 1 << bit) for i in range(n)])]
  transfers between devices with their start and end apart: 3 -> 19, of which waited for: 3 -> 14; matrix products, arithmetic and copies ran while one was open for 7% -> 3% of each run, Pallas kernels for 0% -> 10%
where the time goes in v1:
time: 223 us; the launch traced here: 222 us
  waiting for transfers between devices  91.4 us (41%)
  Pallas kernels  86.9 us (39%)
  starting transfers between devices  29.2 us (13%)
  other arithmetic  8 us (4%)
  local copies, waits for them, and re-layouts  5.93 us (3%)
    ppermute x19, waiting for transfers between devices, flip_bit(): return lax.ppermute(value, axis_name, [(i, i ^ 1 << bit) for i in range(n)])  91.4 us
    pallas_call x1, Pallas kernels, run_dlogits(): pl.pallas_call(functools.partial(dlogits_kernel, vocab_dev, tile, tiles),...  32.5 us
    pallas_call x1, Pallas kernels, run_logits(): pl.pallas_call(functools.partial(logits_kernel, vocab_dev, tile, tiles),...  31.8 us
    ppermute x19, starting transfers between devices, flip_bit(): return lax.ppermute(value, axis_name, [(i, i ^ 1 << bit) for i in range(n)])  29.2 us
    pallas_call x1, Pallas kernels, run_head_grad(): pl.pallas_call(head_grad_kernel, grid=(tiles,), in_specs=[whole((tokens,...  22.6 us
  transfers between devices with their start and end apart: 19, of which 14 were waited for; matrix products, arithmetic and copies ran while one was open for 3% of the time, Pallas kernels for 10%

profile of v1, /device:TPU:0, one launch (start us, length us, event | category | flops | bytes accessed | tf_op | source)
XLA Modules:
  0.0 222.4 jit_solution(17233384244705107227)
XLA Ops:
  0.7 4.1 %collective-permute-start = (bf16[1,32,2048]{2,1,0:T(8,128)(2,1)}, bf16[1,32,2048]{2,1,0:T(8,128)(2,1)S(1)}, u32[]{:S(2)}, u32[]{:S(2)}) collective-permute-start(bf16[1,32,2048]{2,1,0:T(8,128)(2,1)} %param.5), channel_id=1, source_target_pairs={{0,8},{1,9},{2,10},{3,11},{4,12},{5,13},{6,14},{7,15},{8,0},{9,1},... | collective-permute-start | bytes 393224 | tf_op jit(solution)/shard_map/ppermute | solution.py:23
  4.8 6.5 %collective-permute-done = bf16[1,32,2048]{2,1,0:T(8,128)(2,1)S(1)} collective-permute-done((bf16[1,32,2048]{2,1,0:T(8,128)(2,1)}, bf16[1,32,2048]{2,1,0:T(8,128)(2,1)S(1)}, u32[]{:S(2)}, u32[]{:S(2)}) %collective-permute-start) | collective-permute-done | bytes 131104 | tf_op jit(solution)/shard_map/ppermute | solution.py:23
  13.1 6.7 %collective-permute-done.1 = bf16[2,32,2048]{2,1,0:T(8,128)(2,1)S(1)} collective-permute-done((bf16[2,32,2048]{2,1,0:T(8,128)(2,1)S(1)}, bf16[2,32,2048]{2,1,0:T(8,128)(2,1)S(1)}, u32[]{:S(2)}, u32[]{:S(2)}) %collective-permute-start.1) | collective-permute-done | bytes 262176 | tf_op jit(solution)/shard_map/ppermute | solution.py:23
  21.2 10.8 %collective-permute-done.2 = bf16[4,32,2048]{2,1,0:T(8,128)(2,1)S(1)} collective-permute-done((bf16[4,32,2048]{2,1,0:T(8,128)(2,1)S(1)}, bf16[4,32,2048]{2,1,0:T(8,128)(2,1)S(1)}, u32[]{:S(2)}, u32[]{:S(2)}) %collective-permute-start.2) | collective-permute-done | bytes 524320 | tf_op jit(solution)/shard_map/ppermute | solution.py:23
  35.0 19.8 %collective-permute-done.3 = bf16[8,32,2048]{2,1,0:T(8,128)(2,1)S(1)} collective-permute-done((bf16[8,32,2048]{2,1,0:T(8,128)(2,1)S(1)}, bf16[8,32,2048]{2,1,0:T(8,128)(2,1)S(1)}, u32[]{:S(2)}, u32[]{:S(2)}) %collective-permute-start.3) | collective-permute-done | bytes 1048608 | tf_op jit(solution)/shard_map/ppermute | solution.py:23
  54.8 1.6 pad_maximum_fusion
  56.3 31.8 %logits.1 = (bf16[8016,512]{1,0:T(8,128)(2,1)}, bf16[8016,512]{1,0:T(8,128)(2,1)}, bf16[512,2048]{1,0:T(8,128)(2,1)}, f32[8,512]{1,0:T(8,128)}, f32[8,512]{1,0:T(8,128)}) custom-call(bf16[512,2048]{1,0:T(8,128)(2,1)} %bitcast.70, f32[1,2048]{1,0:T(1,128)} %gain_ref.1, s32[1,512]{1,0:T(1,128)} %sub.43.labels_ref, bf16[8016,2048]{1,0:T(8,128)(2,1)} %bitcast.91), custom_call_target="tpu_custom_call" | custom-call | flops 16810770432 | bytes 49250304 | tf_op jit(solution)/shard_map/logits/pallas_call | solution.py:126
  90.4 2.2 collective-permute-done.4
  95.0 2.2 collective-permute-done.5
  97.4 3.2 %collective-permute-start.6 = (f32[3,512]{1,0:T(4,128)S(1)}, f32[3,512]{1,0:T(4,128)S(1)}, u32[]{:S(2)}, u32[]{:S(2)}) collective-permute-start(f32[3,512]{1,0:T(4,128)S(1)} %pad_maximum_fusion.5), channel_id=1, source_target_pairs={{0,4},{1,5},{2,6},{3,7},{4,0},{5,1},{6,2},{7,3},{8,12},{9,13},{10,... | collective-permute-start | bytes 18440 | tf_op jit(solution)/shard_map/ppermute | solution.py:23
  100.6 1.6 collective-permute-done.6
  102.4 4.3 %collective-permute-start.7 = (f32[3,512]{1,0:T(4,128)S(1)}, f32[3,512]{1,0:T(4,128)S(1)}, u32[]{:S(2)}, u32[]{:S(2)}) collective-permute-start(f32[3,512]{1,0:T(4,128)S(1)} %pad_maximum_fusion.6), channel_id=1, source_target_pairs={{0,8},{1,9},{2,10},{3,11},{4,12},{5,13},{6,14},{7,15},{8,0},{9,1},... | collective-permute-start | bytes 18440 | tf_op jit(solution)/shard_map/ppermute | solution.py:23
  106.7 1.6 collective-permute-done.7
  111.3 32.5 %dlogits.1 = (bf16[8016,512]{1,0:T(8,128)(2,1)}, f32[512,2048]{1,0:T(8,128)}, f32[8,512]{1,0:T(8,128)}) custom-call(f32[8,512]{1,0:T(8,128)} %maximum_maximum_fusion.totals_ref, s32[1,512]{1,0:T(1,128)} %sub.43.labels_ref, f32[8,512]{1,0:T(8,128)} %get-tuple-element.12.ms_ref, f32[8,512]{1,0:T(8,128)} %copy-done.3, ...), custom_call_target="tpu_custom_call" | custom-call | flops 16810770432 | bytes 65667072 | tf_op jit(solution)/shard_map/dlogits/pallas_call | solution.py:240
  143.7 1.7 slice.341
  145.5 1.6 collective-permute-start.15
  147.0 23.7 %collective-permute-done.15 = bf16[256,2048]{1,0:T(8,128)(2,1)S(1)} collective-permute-done((bf16[256,2048]{1,0:T(8,128)(2,1)S(1)}, bf16[256,2048]{1,0:T(8,128)(2,1)S(1)}, u32[]{:S(2)}, u32[]{:S(2)}) %collective-permute-start.15) | collective-permute-done | bytes 1048608 | tf_op jit(solution)/shard_map/ppermute | solution.py:23
  170.8 1.9 convert_add_fusion
  172.7 1.6 collective-permute-start.16
  176.5 2.1 collective-permute-done.11
  179.2 6.8 %collective-permute-done.12 = f32[128]{0:T(128)S(1)} collective-permute-done((f32[128]{0:T(128)S(1)}, f32[128]{0:T(128)S(1)}, u32[]{:S(2)}, u32[]{:S(2)}) %collective-permute-start.12) | collective-permute-done | bytes 544 | tf_op jit(solution)/shard_map/ppermute | solution.py:23
  188.3 22.6 %head_grad.1 = bf16[8016,2048]{1,0:T(8,128)(2,1)} custom-call(bf16[512,2048]{1,0:T(8,128)(2,1)} %get-tuple-element.16.normed_ref, bf16[8016,512]{1,0:T(8,128)(2,1)} %get-tuple-element.17.d_ref), custom_call_target="tpu_custom_call" | custom-call | flops 16810770432 | bytes 41041920 | tf_op jit(solution)/shard_map/head_grad/pallas_call | solution.py:284
  211.1 2.9 %collective-permute-start.14 = (f32[32]{0:T(128)S(1)}, f32[32]{0:T(128)S(1)}, u32[]{:S(2)}, u32[]{:S(2)}) collective-permute-start(f32[32]{0:T(128)S(1)} %slice.230), channel_id=1, source_target_pairs={{0,8},{1,9},{2,10},{3,11},{4,12},{5,13},{6,14},{7,15},{8,0},{9,1},... | collective-permute-start | bytes 392 | tf_op jit(solution)/shard_map/ppermute | solution.py:23
  216.0 5.4 %collective-permute-done.18 = bf16[32,2048]{1,0:T(8,128)(2,1)S(1)} collective-permute-done((bf16[32,2048]{1,0:T(8,128)(2,1)S(1)}, bf16[32,2048]{1,0:T(8,128)(2,1)S(1)}, u32[]{:S(2)}, u32[]{:S(2)}) %collective-permute-start.18) | collective-permute-done | bytes 131104 | tf_op jit(solution)/shard_map/ppermute | solution.py:23
  (85 shorter events, 22.2 us)
Async XLA Ops:
  0.6 33.1 %copy-start.4 = (s32[16]{0:T(128)S(1)}, s32[16]{0:T(128)}, u32[]{:S(2)}) copy-start(s32[16]{0:T(128)} %constant.23.clone) | copy-start | bytes 196
  0.6 33.0 %copy-start.2 = (s32[512]{0:T(512)S(1)}, s32[512]{0:T(512)}, u32[]{:S(2)}) copy-start(s32[512]{0:T(512)} %param.8) | copy-start | bytes 6148
  0.7 10.6 %collective-permute-start = (bf16[1,32,2048]{2,1,0:T(8,128)(2,1)}, bf16[1,32,2048]{2,1,0:T(8,128)(2,1)S(1)}, u32[]{:S(2)}, u32[]{:S(2)}) collective-permute-start(bf16[1,32,2048]{2,1,0:T(8,128)(2,1)} %param.5), channel_id=1, source_target_pairs={{0,8},{1,9},{2,10},{3,11},{4,12},{5,13},{6,14},{7,15},{8,0},{9,1},... | collective-permute-start | bytes 393224 | tf_op jit(solution)/shard_map/ppermute | solution.py:23
  12.2 7.6 %collective-permute-start.1 = (bf16[2,32,2048]{2,1,0:T(8,128)(2,1)S(1)}, bf16[2,32,2048]{2,1,0:T(8,128)(2,1)S(1)}, u32[]{:S(2)}, u32[]{:S(2)}) collective-permute-start(bf16[2,32,2048]{2,1,0:T(8,128)(2,1)S(1)} %get-tuple-element.28), channel_id=1, source_target_pairs={{0,4},{1,5},{2,6},{3,7},{4,0},{5,1},{6,2},{7,3},{8,12},{9,13},{10,... | collective-permute-start | bytes 786440 | tf_op jit(solution)/shard_map/ppermute | solution.py:23
  19.8 12.3 %collective-permute-start.2 = (bf16[4,32,2048]{2,1,0:T(8,128)(2,1)S(1)}, bf16[4,32,2048]{2,1,0:T(8,128)(2,1)S(1)}, u32[]{:S(2)}, u32[]{:S(2)}) collective-permute-start(bf16[4,32,2048]{2,1,0:T(8,128)(2,1)S(1)} %bitcast.71), channel_id=1, source_target_pairs={{0,2},{1,3},{2,0},{3,1},{4,6},{5,7},{6,4},{7,5},{8,10},{9,11},{10,... | collective-permute-start | bytes 1572872 | tf_op jit(solution)/shard_map/ppermute | solution.py:23
  32.2 22.6 %collective-permute-start.3 = (bf16[8,32,2048]{2,1,0:T(8,128)(2,1)S(1)}, bf16[8,32,2048]{2,1,0:T(8,128)(2,1)S(1)}, u32[]{:S(2)}, u32[]{:S(2)}) collective-permute-start(bf16[8,32,2048]{2,1,0:T(8,128)(2,1)S(1)} %bitcast.68), channel_id=1, source_target_pairs={{0,1},{1,0},{2,3},{3,2},{4,5},{5,4},{6,7},{7,6},{8,9},{9,8},{10,11... | collective-permute-start | bytes 3145736 | tf_op jit(solution)/shard_map/ppermute | solution.py:23
  88.2 22.5 %collective-permute-start.10 = (bf16[8016,512]{1,0:T(8,128)(2,1)}, bf16[8016,512]{1,0:T(8,128)(2,1)}, u32[]{:S(2)}, u32[]{:S(2)}) collective-permute-start(bf16[8016,512]{1,0:T(8,128)(2,1)} %get-tuple-element.13.ps_ref), channel_id=1, source_target_pairs={{0,16},{16,0},{1,17},{17,1},{2,18},{18,2},{3,19},{19,3},{4,20},{20... | collective-permute-start | bytes 24625160 | tf_op jit(solution)/shard_map/ppermute | solution.py:23
  89.0 3.7 %collective-permute-start.4 = (f32[3,512]{1,0:T(4,128)S(1)}, f32[3,512]{1,0:T(4,128)S(1)}, u32[]{:S(2)}, u32[]{:S(2)}) collective-permute-start(f32[3,512]{1,0:T(4,128)S(1)} %slice.192), channel_id=1, source_target_pairs={{0,1},{1,0},{2,3},{3,2},{4,5},{5,4},{6,7},{7,6},{8,9},{9,8},{10,11... | collective-permute-start | bytes 18440 | tf_op jit(solution)/shard_map/ppermute | solution.py:23
  93.5 3.7 %collective-permute-start.5 = (f32[3,512]{1,0:T(4,128)S(1)}, f32[3,512]{1,0:T(4,128)S(1)}, u32[]{:S(2)}, u32[]{:S(2)}) collective-permute-start(f32[3,512]{1,0:T(4,128)S(1)} %pad_maximum_fusion.4), channel_id=1, source_target_pairs={{0,2},{1,3},{2,0},{3,1},{4,6},{5,7},{6,4},{7,5},{8,10},{9,11},{10,... | collective-permute-start | bytes 18440 | tf_op jit(solution)/shard_map/ppermute | solution.py:23
  97.4 4.9 %collective-permute-start.6 = (f32[3,512]{1,0:T(4,128)S(1)}, f32[3,512]{1,0:T(4,128)S(1)}, u32[]{:S(2)}, u32[]{:S(2)}) collective-permute-start(f32[3,512]{1,0:T(4,128)S(1)} %pad_maximum_fusion.5), channel_id=1, source_target_pairs={{0,4},{1,5},{2,6},{3,7},{4,0},{5,1},{6,2},{7,3},{8,12},{9,13},{10,... | collective-permute-start | bytes 18440 | tf_op jit(solution)/shard_map/ppermute | solution.py:23
  102.4 5.9 %collective-permute-start.7 = (f32[3,512]{1,0:T(4,128)S(1)}, f32[3,512]{1,0:T(4,128)S(1)}, u32[]{:S(2)}, u32[]{:S(2)}) collective-permute-start(f32[3,512]{1,0:T(4,128)S(1)} %pad_maximum_fusion.6), channel_id=1, source_target_pairs={{0,8},{1,9},{2,10},{3,11},{4,12},{5,13},{6,14},{7,15},{8,0},{9,1},... | collective-permute-start | bytes 18440 | tf_op jit(solution)/shard_map/ppermute | solution.py:23
  108.8 1.2 collective-permute-start.8
  108.9 1.7 collective-permute-start.9
  110.7 0.6 copy-start.3
  145.5 25.3 %collective-permute-start.15 = (bf16[256,2048]{1,0:T(8,128)(2,1)S(1)}, bf16[256,2048]{1,0:T(8,128)(2,1)S(1)}, u32[]{:S(2)}, u32[]{:S(2)}) collective-permute-start(bf16[256,2048]{1,0:T(8,128)(2,1)S(1)} %slice.341), channel_id=1, source_target_pairs={{0,1},{1,0},{2,3},{3,2},{4,5},{5,4},{6,7},{7,6},{8,9},{9,8},{10,11... | collective-permute-start | bytes 3145736 | tf_op jit(solution)/shard_map/ppermute | solution.py:23
  172.7 14.5 %collective-permute-start.16 = (bf16[128,2048]{1,0:T(8,128)(2,1)S(1)}, bf16[128,2048]{1,0:T(8,128)(2,1)S(1)}, u32[]{:S(2)}, u32[]{:S(2)}) collective-permute-start(bf16[128,2048]{1,0:T(8,128)(2,1)S(1)} %slice.342), channel_id=1, source_target_pairs={{0,2},{1,3},{2,0},{3,1},{4,6},{5,7},{6,4},{7,5},{8,10},{9,11},{10,... | collective-permute-start | bytes 1572872 | tf_op jit(solution)/shard_map/ppermute | solution.py:23
  175.0 3.6 %collective-permute-start.11 = (f32[256]{0:T(256)S(1)}, f32[256]{0:T(256)S(1)}, u32[]{:S(2)}, u32[]{:S(2)}) collective-permute-start(f32[256]{0:T(256)S(1)} %bitcast.90), channel_id=1, source_target_pairs={{0,1},{1,0},{2,3},{3,2},{4,5},{5,4},{6,7},{7,6},{8,9},{9,8},{10,11... | collective-permute-start | bytes 3080 | tf_op jit(solution)/shard_map/ppermute | solution.py:23
  178.6 7.4 %collective-permute-start.12 = (f32[128]{0:T(128)S(1)}, f32[128]{0:T(128)S(1)}, u32[]{:S(2)}, u32[]{:S(2)}) collective-permute-start(f32[128]{0:T(128)S(1)} %slice.226), channel_id=1, source_target_pairs={{0,2},{1,3},{2,0},{3,1},{4,6},{5,7},{6,4},{7,5},{8,10},{9,11},{10,... | collective-permute-start | bytes 1544 | tf_op jit(solution)/shard_map/ppermute | solution.py:23
  186.1 24.9 %collective-permute-start.13 = (f32[64]{0:T(128)S(1)}, f32[64]{0:T(128)S(1)}, u32[]{:S(2)}, u32[]{:S(2)}) collective-permute-start(f32[64]{0:T(128)S(1)} %slice.228), channel_id=1, source_target_pairs={{0,4},{1,5},{2,6},{3,7},{4,0},{5,1},{6,2},{7,3},{8,12},{9,13},{10,... | collective-permute-start | bytes 776 | tf_op jit(solution)/shard_map/ppermute | solution.py:23
  187.4 26.6 %collective-permute-start.17 = (bf16[64,2048]{1,0:T(8,128)(2,1)S(1)}, bf16[64,2048]{1,0:T(8,128)(2,1)S(1)}, u32[]{:S(2)}, u32[]{:S(2)}) collective-permute-start(bf16[64,2048]{1,0:T(8,128)(2,1)S(1)} %slice.343), channel_id=1, source_target_pairs={{0,4},{1,5},{2,6},{3,7},{4,0},{5,1},{6,2},{7,3},{8,12},{9,13},{10,... | collective-permute-start | bytes 786440 | tf_op jit(solution)/shard_map/ppermute | solution.py:23
  188.3 33.1 %copy-start = (bf16[1,32,2048]{2,1,0:T(8,128)(2,1)S(1)}, bf16[1,32,2048]{2,1,0:T(8,128)(2,1)}, u32[]{:S(2)}) copy-start(bf16[1,32,2048]{2,1,0:T(8,128)(2,1)} %param.5) | copy-start | bytes 393220
  188.3 33.1 %copy-start.1 = (f32[1,2048]{1,0:T(1,128)S(1)}, f32[1,2048]{1,0:T(1,128)}, u32[]{:S(2)}) copy-start(f32[1,2048]{1,0:T(1,128)} %gain_ref.1) | copy-start | bytes 24580
  211.1 4.5 %collective-permute-start.14 = (f32[32]{0:T(128)S(1)}, f32[32]{0:T(128)S(1)}, u32[]{:S(2)}, u32[]{:S(2)}) collective-permute-start(f32[32]{0:T(128)S(1)} %slice.230), channel_id=1, source_target_pairs={{0,8},{1,9},{2,10},{3,11},{4,12},{5,13},{6,14},{7,15},{8,0},{9,1},... | collective-permute-start | bytes 392 | tf_op jit(solution)/shard_map/ppermute | solution.py:23
  214.1 7.3 %collective-permute-start.18 = (bf16[32,2048]{1,0:T(8,128)(2,1)S(1)}, bf16[32,2048]{1,0:T(8,128)(2,1)S(1)}, u32[]{:S(2)}, u32[]{:S(2)}) collective-permute-start(bf16[32,2048]{1,0:T(8,128)(2,1)S(1)} %slice.344), channel_id=1, source_target_pairs={{0,8},{1,9},{2,10},{3,11},{4,12},{5,13},{6,14},{7,15},{8,0},{9,1},... | collective-permute-start | bytes 393224 | tf_op jit(solution)/shard_map/ppermute | solution.py:23

commit v2 on v1

v2 whole, which is shorter than its diff:
```python
import functools
import jax
import jax.numpy as jnp
from jax import lax
from jax.experimental import pallas as pl
from jax.experimental.pallas import tpu as pltpu
from jax.sharding import PartitionSpec as P

EPS = 1e-05
BETA = 0.5
TILE = 1024
CHUNK = 128
LANES = 128
VMEM_SHARED = 24 * 1024 * 1024
VMEM_ALONE = 40 * 1024 * 1024
GRAD_EDGES = (0, 3, 5, 8)
LOAD_COPIES = 4
SMALL = pl.CostEstimate(flops=4096, bytes_accessed=4096, transcendentals=0)


def cdiv(a, b):
    return -(-a // b)


def tiling(vocab_dev):
    tile = min(TILE, vocab_dev)
    return tile, cdiv(vocab_dev, tile)


def whole(shape):
    return pl.BlockSpec(shape, lambda j: (0, 0))


def whole_vmem():
    return pl.BlockSpec(memory_space=pltpu.VMEM)


def pinned(value):
    return pltpu.with_memory_space_constraint(value, pltpu.VMEM)


def chunks(valid):
    return [(start, min(CHUNK, valid - start)) for start in range(0, valid, CHUNK)]


def pick_row(table, index):
    here = lax.broadcasted_iota(jnp.int32, table.shape, 0) == index
    return jnp.sum(jnp.where(here, table, 0.0), axis=0, keepdims=True)


def load_kernel(first, rows, w_ref, *refs):
    out_ref, sems = refs[-2:]
    pieces = []
    step = cdiv(cdiv(rows, LOAD_COPIES), 16) * 16
    for i, start in enumerate(range(0, rows, step)):
        piece = pl.ds(first + start, min(step, rows - start))
        pieces.append(pltpu.make_async_copy(w_ref.at[piece, :], out_ref.at[piece, :], sems.at[i]))
    for piece in pieces:
        piece.start()
    for piece in pieces:
        piece.wait()


def run_load(first, rows, weights, after, held):
    operands, in_specs, aliases = [weights, after], [pl.BlockSpec(memory_space=pl.ANY)] * 2, {}
    if held is not None:
        operands.append(held)
        in_specs.append(whole_vmem())
        aliases[2] = 0
    return pl.pallas_call(
        functools.partial(load_kernel, first, rows),
        in_specs=in_specs,
        out_specs=whole_vmem(),
        out_shape=pltpu.VMEM(weights.shape, weights.dtype),
        scratch_shapes=[pltpu.SemaphoreType.DMA((LOAD_COPIES,))],
        input_output_aliases=aliases,
        compiler_params=pltpu.CompilerParams(vmem_limit_bytes=VMEM_SHARED),
        cost_estimate=pl.CostEstimate(flops=0, bytes_accessed=4 * rows * weights.shape[1], transcendentals=0),
        name="load",
    )(*operands)


def join_kernel(count, split, *refs):
    pieces, outs = refs[:count], refs[-2 if split else -1 :]
    for i, piece in enumerate(pieces):
        half = piece.shape[0] // 2
        for part in range(2):
            rows = piece[part * half : (part + 1) * half, :]
            if split:
                outs[part][i * half : (i + 1) * half, :] = rows
            else:
                place = (part * count + i) * half
                outs[0][place : place + half, :] = rows


def run_join(pieces, split, weights):
    rows, width = pieces[0].shape
    total = rows * len(pieces)
    kind = lambda n: jax.ShapeDtypeStruct((n, width), pieces[0].dtype)
    return pl.pallas_call(
        functools.partial(join_kernel, len(pieces), split),
        in_specs=[whole_vmem()] * (len(pieces) + 1),
        out_specs=[whole_vmem()] * (2 if split else 1),
        out_shape=[kind(total // 2)] * 2 if split else [kind(total)],
        compiler_params=pltpu.CompilerParams(vmem_limit_bytes=VMEM_SHARED),
        cost_estimate=SMALL,
        name="join",
    )(*pieces, weights)


def stack_kernel(w_ref, low_a, high_a, low_b, high_b, a_ref, b_ref):
    half = low_a.shape[0]
    for low, high, out in ((low_a, high_a, a_ref), (low_b, high_b, b_ref)):
        out[:half, :] = low[...]
        out[half:, :] = high[...]


def run_stack(weights, *pieces):
    rows, width = pieces[0].shape
    return pl.pallas_call(
        stack_kernel,
        in_specs=[whole_vmem()] * 5,
        out_specs=[whole_vmem()] * 2,
        out_shape=[jax.ShapeDtypeStruct((2 * rows, width), pieces[0].dtype)] * 2,
        cost_estimate=SMALL,
        compiler_params=pltpu.CompilerParams(vmem_limit_bytes=VMEM_SHARED),
        name="stack",
    )(weights, *pieces)


def merge_kernel(count, lanes, final, table_ref, *refs):
    arrived, out_ref = refs[:count], refs[-1]
    tokens = table_ref.shape[1]
    lane = lax.broadcasted_iota(jnp.int32, (8, tokens), 1)

    def swap(value, stride):
        return jnp.where(
            lane & stride == 0, pltpu.roll(value, tokens - stride, 1), pltpu.roll(value, stride, 1)
        )

    tables = [table_ref[...]]
    for ref, moves in zip(arrived, lanes):
        value = ref[...]
        for stride_a, stride_b, part in moves:
            if stride_a == stride_b:
                value = swap(value, stride_a)
            else:
                value = jnp.where(lane & part == 0, swap(value, stride_a), swap(value, stride_b))
        tables.append(value)
    top = functools.reduce(jnp.maximum, [t[0:1] for t in tables])
    total = sum(t[1:2] * jnp.exp(t[0:1] - top) for t in tables)
    picked = sum(t[2:3] for t in tables)
    out_ref[0:8, :] = jnp.zeros((8, tokens), jnp.float32)
    if final:
        out_ref[0:1, :] = top + jnp.log(total)
        out_ref[1:2, :] = picked
        out_ref[8:, :] = refs[count][...]
    else:
        out_ref[0:1, :] = top
        out_ref[1:2, :] = total
        out_ref[2:3, :] = picked


def run_merge(weights, table, arrived, lanes, tops):
    operands = [table, *arrived] + ([] if tops is None else [tops]) + [weights]
    rows = 8 + (0 if tops is None else tops.shape[0])
    return pl.pallas_call(
        functools.partial(merge_kernel, len(arrived), lanes, tops is not None),
        in_specs=[whole_vmem()] * len(operands),
        out_specs=whole_vmem(),
        out_shape=jax.ShapeDtypeStruct((rows, table.shape[1]), jnp.float32),
        compiler_params=pltpu.CompilerParams(vmem_limit_bytes=VMEM_SHARED),
        cost_estimate=SMALL,
        name="totals",
    )(*operands)


def logits_kernel(
    tile, tiles, group_index, rows_a_ref, rows_b_ref, gain_ref, labels_ref, w_ref, *refs
):
    p_ref, l_ref, normed_ref, tops_ref, stats_ref, logits_ref, m_ref, s_ref, picked_ref = refs[-9:]
    step = pl.program_id(0)
    tokens = normed_ref.shape[0]
    last_rows = w_ref.shape[0] - (tiles - 1) * tile

    def matmul(slot, start, rows):
        logits_ref[slot, :rows, :] = lax.dot_general(
            w_ref[pl.ds(start, rows), :], normed_ref[...], (((1,), (1,)), ((), ())),
            preferred_element_type=jnp.float32,
        )

    def soften(slot, index, valid_rows):
        group = min(tokens, LANES)
        for col in range(0, tokens, group):
            cols = slice(col, col + group)
            target = labels_ref[:, group_index * tokens + col : group_index * tokens + col + group] - index * tile
            top = None
            for start, rows in chunks(valid_rows):
                part = jnp.max(logits_ref[slot, start : start + rows, cols], axis=0, keepdims=True)
                top = part if top is None else jnp.maximum(top, part)
            total = jnp.zeros((1, group), jnp.float32)
            picked = picked_ref[:, cols]
            for start, rows in chunks(valid_rows):
                values = logits_ref[slot, start : start + rows, cols]
                row = lax.broadcasted_iota(jnp.int32, (rows, group), 0)
                lowered = values - top
                exps = jnp.exp(lowered)
                l_ref[start : start + rows, cols] = lowered.astype(l_ref.dtype)
                p_ref[start : start + rows, cols] = exps.astype(p_ref.dtype)
                chosen = jnp.where(row == target - start, values, 0.0)
                total = total + jnp.sum(exps, axis=0, keepdims=True)
                picked = picked + jnp.sum(chosen, axis=0, keepdims=True)
            here = lax.broadcasted_iota(jnp.int32, (m_ref.shape[0], group), 0) == index
            m_ref[:, cols] = jnp.where(here, top, m_ref[:, cols])
            s_ref[:, cols] = jnp.where(here, total, s_ref[:, cols])
            picked_ref[:, cols] = picked

    @pl.when(step == 0)
    def _():
        half = tokens // 2
        for place, rows_ref in ((0, rows_a_ref), (half, rows_b_ref)):
            values = rows_ref[...].astype(jnp.float32)
            inverse = lax.rsqrt(jnp.mean(values * values, axis=-1, keepdims=True) + EPS)
            normed_ref[place : place + half, :] = (values * inverse * gain_ref[...]).astype(jnp.bfloat16)
        m_ref[...] = jnp.full_like(m_ref, -jnp.inf)
        s_ref[...] = jnp.zeros_like(s_ref)
        picked_ref[...] = jnp.zeros_like(picked_ref)
        matmul(0, 0, last_rows if tiles == 1 else tile)

    if tiles > 2:

        @pl.when((step > 0) & (step < tiles - 1))
        def _():
            matmul(lax.rem(step, 2), pl.multiple_of(step * tile, tile), tile)
            soften(lax.rem(step + 1, 2), step - 1, tile)

    if tiles > 1:

        @pl.when(step == tiles - 1)
        def _():
            matmul((tiles - 1) % 2, (tiles - 1) * tile, last_rows)
            soften(tiles % 2, tiles - 2, tile)

    @pl.when(step == tiles)
    def _():
        soften((tiles - 1) % 2, tiles - 1, last_rows)
        tops = m_ref[...]
        top = jnp.max(tops, axis=0, keepdims=True)
        total = jnp.sum(s_ref[...] * jnp.exp(tops - top), axis=0, keepdims=True)
        place = group_index * tokens
        cols = slice(place, place + tokens)
        if group_index:
            stats_ref[:, :place] = refs[1][...]
            tops_ref[:, :place] = refs[2][...]
        tops_ref[:, cols] = tops
        stats_ref[:, cols] = jnp.zeros((8, tokens), jnp.float32)
        stats_ref[0:1, cols] = top
        stats_ref[1:2, cols] = total
        stats_ref[2:3, cols] = picked_ref[...]


def run_logits(group, rows_a, rows_b, gain, labels, weights, before):
    half, width = rows_a.shape
    tokens = 2 * half
    vocab_dev = weights.shape[0]
    tile, tiles = tiling(vocab_dev)
    groups = cdiv(tiles, 8) * 8
    behind = pl.BlockSpec((tile, tokens), lambda j: (jnp.maximum(j - 1, 0), 0))
    operands = [rows_a, rows_b, gain, labels, weights]
    in_specs = [
        whole_vmem(),
        whole_vmem(),
        whole((1, width)),
        whole_vmem(),
        whole_vmem(),
    ]
    aliases = {}
    if group:
        aliases[len(operands)] = 2
        operands += before
        in_specs += [pl.BlockSpec(memory_space=pl.ANY), whole_vmem(), whole_vmem()]
    return pl.pallas_call(
        functools.partial(logits_kernel, tile, tiles, group),
        grid=(tiles + 1,),
        in_specs=in_specs,
        out_specs=[
            behind,
            behind,
            pl.BlockSpec((tokens, width), lambda j: (group, 0)),
            whole_vmem(),
            whole_vmem(),
        ],
        out_shape=[
            jax.ShapeDtypeStruct((vocab_dev, tokens), jnp.bfloat16),
            jax.ShapeDtypeStruct((vocab_dev, tokens), jnp.bfloat16),
            jax.ShapeDtypeStruct((2 * tokens, width), jnp.bfloat16),
            jax.ShapeDtypeStruct((groups, (group + 1) * tokens), jnp.float32),
            jax.ShapeDtypeStruct((8, (group + 1) * tokens), jnp.float32),
        ],
        scratch_shapes=[
            pltpu.VMEM((2, tile, tokens), jnp.float32),
            pltpu.VMEM((groups, tokens), jnp.float32),
            pltpu.VMEM((groups, tokens), jnp.float32),
            pltpu.VMEM((1, tokens), jnp.float32),
        ],
        input_output_aliases=aliases,
        compiler_params=pltpu.CompilerParams(vmem_limit_bytes=VMEM_SHARED),
        cost_estimate=pl.CostEstimate(
            flops=2 * tokens * width * vocab_dev,
            bytes_accessed=4 * tokens * vocab_dev,
            transcendentals=tokens * vocab_dev,
        ),
        name="logits",
    )(*operands)


def dlogits_kernel(
    tile, tiles, group_index, own_ref, other_ref, labels_ref, ps_ref, pt_ref, l_ref, w_ref, *refs
):
    d_ref, first_ref, second_ref, up_ref, d_scratch, a_ref, b_ref, g_ref, c_ref = refs[-9:]
    step = pl.program_id(0)
    tokens = ps_ref.shape[1]
    all_tokens = labels_ref.shape[1]
    first = group_index * tokens
    scale = 1.0 / all_tokens
    last_rows = w_ref.shape[0] - (tiles - 1) * tile

    def weigh(slot, index, valid_rows):
        group = min(tokens, LANES)
        for col in range(0, tokens, group):
            cols = slice(col, col + group)
            target = labels_ref[:, first + col : first + col + group] - index * tile
            own, other, gap = (pick_row(ref[:, cols], index) for ref in (a_ref, b_ref, g_ref))
            cross = c_ref[:, cols]
            for start, rows in chunks(valid_rows):
                here = slice(start, start + rows)
                row = lax.broadcasted_iota(jnp.int32, (rows, group), 0)
                student = ps_ref[here, cols].astype(jnp.float32) * own
                teacher = pt_ref[here, cols].astype(jnp.float32) * other
                lowered = l_ref[here, cols].astype(jnp.float32)
                part = teacher * (gap - lowered)
                value = student - teacher - jnp.where(row == target - start, scale, 0.0)
                cross = cross + jnp.sum(part, axis=0, keepdims=True)
                value = value.astype(jnp.bfloat16)
                d_ref[here, cols] = value
                d_scratch[slot, here, cols] = value
            c_ref[:, cols] = cross

    def matmul(slot, start, rows):
        for out in range(0, up_ref.shape[1], 512):
            cols = slice(out, out + 512)
            up_ref[:, cols] += lax.dot_general(
                d_scratch[slot, :rows, :], w_ref[pl.ds(start, rows), cols], (((0,), (0,)), ((), ())),
                preferred_element_type=jnp.float32,
            )

    @pl.when(step == 0)
    def _():
        here = slice(first, first + tokens)
        own_total, other_total = own_ref[0:1, here], other_ref[0:1, here]
        a_ref[...] = jnp.exp(own_ref[8:, here] - own_total) * ((1.0 + BETA) * scale)
        b_ref[...] = jnp.exp(other_ref[8:, here] - other_total) * (BETA * scale)
        g_ref[...] = own_total - own_ref[8:, here]
        c_ref[...] = jnp.zeros_like(c_ref)
        up_ref[...] = jnp.zeros_like(up_ref)
        weigh(0, 0, last_rows if tiles == 1 else tile)

    if tiles > 2:

        @pl.when((step > 0) & (step < tiles - 1))
        def _():
            matmul(lax.rem(step + 1, 2), pl.multiple_of((step - 1) * tile, tile), tile)
            weigh(lax.rem(step, 2), step, tile)

    if tiles > 1:

        @pl.when(step == tiles - 1)
        def _():
            matmul(tiles % 2, (tiles - 2) * tile, tile)
            weigh((tiles - 1) % 2, tiles - 1, last_rows)

    @pl.when(step == tiles)
    def _():
        matmul((tiles - 1) % 2, (tiles - 1) * tile, last_rows)
        width = up_ref.shape[1]
        half = tokens // 2
        column = jnp.broadcast_to(c_ref[...] * (all_tokens / BETA), (LANES, tokens)).T
        lane = lax.broadcasted_iota(jnp.int32, (tokens, LANES), 1)
        if first_ref.dtype == jnp.float32:
            edge = jnp.where(lane == 0, column, 0.0)
        else:
            high = column.astype(jnp.bfloat16).astype(jnp.float32)
            edge = jnp.where(lane == 0, high, jnp.where(lane == 1, column - high, 0.0))
        for ref, place in ((first_ref, 0), (second_ref, half)):
            ref[:, :width] = up_ref[place : place + half, :].astype(ref.dtype)
            ref[:, width:] = edge[place : place + half, :].astype(ref.dtype)


def run_dlogits(group, totals, other_totals, labels, p_own, p_other, lowered, weights, dlogits, out_type):
    tokens = p_own.shape[1]
    vocab_dev, width = weights.shape
    tile, tiles = tiling(vocab_dev)
    groups = totals.shape[0] - 8
    wide = width + LANES
    ahead = lambda j: jnp.minimum(j, tiles - 1)
    here = pl.BlockSpec((tile, tokens), lambda j: (ahead(j), 0))
    p_own, p_other, lowered = (pltpu.with_memory_space_constraint(v, pltpu.HBM) for v in (p_own, p_other, lowered))
    operands = [totals, other_totals, labels, p_own, p_other, lowered, weights]
    in_specs = [
        whole_vmem(),
        whole_vmem(),
        whole_vmem(),
        here,
        here,
        here,
        pl.BlockSpec(memory_space=pltpu.VMEM),
    ]
    aliases = {}
    if dlogits is not None:
        aliases[len(operands)] = 0
        operands.append(dlogits)
        in_specs.append(pl.BlockSpec(memory_space=pl.ANY))
    return pl.pallas_call(
        functools.partial(dlogits_kernel, tile, tiles, group),
        grid=(tiles + 1,),
        in_specs=in_specs,
        out_specs=[
            pl.BlockSpec((tile, tokens), lambda j: (ahead(j), group)),
            whole_vmem(),
            whole_vmem(),
        ],
        out_shape=[
            jax.ShapeDtypeStruct((vocab_dev, 2 * tokens), jnp.bfloat16),
            jax.ShapeDtypeStruct((tokens // 2, wide), out_type),
            jax.ShapeDtypeStruct((tokens // 2, wide), out_type),
        ],
        scratch_shapes=[
            pltpu.VMEM((tokens, width), jnp.float32),
            pltpu.VMEM((2, tile, tokens), jnp.bfloat16),
            pltpu.VMEM((groups, tokens), jnp.float32),
            pltpu.VMEM((groups, tokens), jnp.float32),
            pltpu.VMEM((groups, tokens), jnp.float32),
            pltpu.VMEM((1, tokens), jnp.float32),
        ],
        input_output_aliases=aliases,
        compiler_params=pltpu.CompilerParams(vmem_limit_bytes=VMEM_SHARED),
        cost_estimate=pl.CostEstimate(
            flops=2 * tokens * width * vocab_dev,
            bytes_accessed=8 * tokens * vocab_dev,
            transcendentals=0,
        ),
        name="dlogits",
    )(*operands)


def fold_kernel(count, gots, sends, *refs):
    sums, arrived, outs = refs[:count], refs[count : count + gots], refs[-1 - sends :]
    keep, send = outs[0], outs[1:]
    width = keep.shape[2] - LANES
    cut = keep.shape[1]
    lane = lax.broadcasted_iota(jnp.int32, (cut, LANES), 1)
    for part in range(2):
        held = sums[part][...] if count == 2 else sums[0][part]
        got = arrived[part][...] if gots == 2 else arrived[0][part]
        total = held + got.astype(jnp.float32)
        keep[part] = total[:cut]
        gone = total[cut:]
        cross = gone[:, width : width + 1] + gone[:, width + 1 : width + 2]
        high = cross.astype(jnp.bfloat16).astype(jnp.float32)
        edge = jnp.where(lane == 0, high, jnp.where(lane == 1, cross - high, 0.0))
        value = jnp.concatenate([gone[:, :width], edge], axis=1).astype(jnp.bfloat16)
        if sends == 2:
            send[part][...] = value
        else:
            send[0][part] = value


def run_fold(sums, arrived, sends, after):
    rows, wide = sums[0].shape[-2:]
    cut = rows // 2
    operands = list(sums) + list(arrived)
    in_specs = [pl.BlockSpec(memory_space=pltpu.VMEM)] * len(operands)
    if after is not None:
        operands.append(pltpu.with_memory_space_constraint(after, pltpu.HBM))
        in_specs.append(pl.BlockSpec(memory_space=pl.ANY))
    shape = (cut, wide) if sends == 2 else (2, cut, wide)
    return pl.pallas_call(
        functools.partial(fold_kernel, len(sums), len(arrived), sends),
        in_specs=in_specs,
        out_specs=[pl.BlockSpec(memory_space=pltpu.VMEM)] * (1 + sends),
        out_shape=[jax.ShapeDtypeStruct((2, cut, wide), jnp.float32)]
        + [jax.ShapeDtypeStruct(shape, jnp.bfloat16)] * sends,
        compiler_params=pltpu.CompilerParams(vmem_limit_bytes=VMEM_SHARED),
        cost_estimate=SMALL,
        name="fold",
    )(*operands)


def head_grad_kernel(normed_ref, d_ref, *refs):
    out_ref = refs[-1]
    out_ref[...] = jnp.dot(d_ref[...], normed_ref[...], preferred_element_type=jnp.float32).astype(out_ref.dtype)


def run_head_grad(first, count, normed, dlogits, grad, after):
    tokens, width = normed.shape
    vocab_dev = dlogits.shape[0]
    tile, tiles = tiling(vocab_dev)
    operands = [normed, pltpu.with_memory_space_constraint(dlogits, pltpu.HBM)]
    in_specs = [whole((tokens, width)), pl.BlockSpec((tile, tokens), lambda j: (first + j, 0))]
    aliases = {}
    for value in after:
        operands.append(value)
        in_specs.append(pl.BlockSpec(memory_space=pl.ANY))
    if grad is not None:
        aliases[len(operands)] = 0
        operands.append(pltpu.with_memory_space_constraint(grad, pltpu.HBM))
        in_specs.append(pl.BlockSpec(memory_space=pl.ANY))
    return pl.pallas_call(
        head_grad_kernel,
        grid=(count,),
        in_specs=in_specs,
        out_specs=pl.BlockSpec((tile, width), lambda j: (first + j, 0)),
        out_shape=jax.ShapeDtypeStruct((vocab_dev, width), jnp.bfloat16),
        input_output_aliases=aliases,
        compiler_params=pltpu.CompilerParams(vmem_limit_bytes=VMEM_ALONE),
        cost_estimate=pl.CostEstimate(
            flops=2 * tokens * width * tile * count,
            bytes_accessed=2 * width * tile * count + 2 * tokens * tile * count,
            transcendentals=0,
        ),
        name="head_grad",
    )(*operands)


def moved(value, offset):
    n = lax.axis_size("fsdp")
    return lax.ppermute(value, "fsdp", [(i, i ^ offset) for i in range(n)])


def other_member(value):
    return lax.ppermute(value, "member", [(0, 1), (1, 0)])


def token_order(bits):
    offsets = [0]
    for bit in reversed(range(2, bits)):
        offsets = offsets + [o | 1 << bit for o in offsets]
    order = []
    for group in range(2):
        for half in range(2):
            group_bit, place_bit = (1, 2) if half == 0 else (2, 1)
            for place in range(2):
                order += [(group * group_bit + place * place_bit + o, half) for o in offsets]
    return order


def lane_moves(offset, bits, half):
    moves = []
    for bit in range(bits):
        if offset >> bit & 1:
            group, place = half << bits, half << (bits - 2)
            strides = {0: (group, place), 1: (place, group)}.get(bit, (half << (bits - 1 - bit),) * 2)
            moves.append(strides + (half << (bits - 1),))
    return tuple(moves)


def pack(value, width):
    cross = value[..., width : width + 1] + value[..., width + 1 : width + 2]
    high = lax.reduce_precision(cross, 8, 7)
    rest = jnp.zeros(value.shape[:-1] + (LANES - 2,), jnp.float32)
    return jnp.concatenate([value[..., :width], high, cross - high, rest], axis=-1).astype(jnp.bfloat16)


def body(hidden, gain, head, labels):
    own_rows = hidden[0]
    gain_row = gain[0]
    tok_dev, width = own_rows.shape
    vocab_dev = head.shape[2]
    count = lax.axis_size("fsdp")
    bits = count.bit_length() - 1
    index = lax.axis_index("fsdp")
    half = tok_dev // 2
    tokens = tok_dev * count

    order = token_order(bits)
    offsets = jnp.asarray([o for o, _ in order], jnp.int32)
    halves = jnp.asarray([s for _, s in order], jnp.int32)
    local_labels = labels.reshape(2 * count, half)[(offsets ^ index) * 2 + halves].reshape(1, tokens)
    local_labels = local_labels - index * vocab_dev

    first_rows = min(vocab_dev, cdiv(vocab_dev // 2, 16) * 16)
    weights = pinned(run_load(0, first_rows, head[0].T, local_labels, None))
    held = [own_rows]
    for bit in reversed(range(2, bits)):
        held = run_join([held[0], moved(held[0], 1 << bit)], bit == 2, weights)
        if bit == bits - 1 and first_rows < vocab_dev:
            weights = pinned(run_load(first_rows, vocab_dev - first_rows, head[0].T, held[0], weights))
    near_a, near_b = run_stack(weights, held[0], moved(held[0], 2), held[1], moved(held[1], 1))
    far_a = moved(near_a, 1)
    far_b = moved(near_b, 2)

    p_near, l_near, normed, tops, stats = run_logits(
        0, near_a, near_b, gain_row[None], local_labels, weights, []
    )
    p_near_other = other_member(p_near)
    p_far, l_far, normed, tops, table = run_logits(
        1, far_a, far_b, gain_row[None], local_labels, weights, [normed, stats, tops]
    )
    p_far_other = other_member(p_far)

    for bit in range(0, bits, 2):
        steps = [k << bit for k in range(1, 4) if k << bit < count]
        lanes = [lane_moves(k, bits, half) for k in steps]
        table = run_merge(weights, table, [moved(table, k) for k in steps], lanes, tops if bit + 2 >= bits else None)
    other_totals = other_member(table)

    dlogits, send_a, send_b = run_dlogits(
        1, table, other_totals, local_labels, p_far, p_far_other, l_far, weights, None, jnp.bfloat16
    )
    got_a, got_b = moved(send_a, 1), moved(send_b, 2)
    dlogits, sum_a, sum_b = run_dlogits(
        0, table, other_totals, local_labels, p_near, p_near_other, l_near, weights, dlogits, jnp.float32
    )

    tile, tiles = tiling(vocab_dev)
    edges = [tiles * i // 8 for i in GRAD_EDGES]
    grad = None
    summed, sends = run_fold((sum_a, sum_b), (got_a, got_b), 2, None), 2
    for step in range(1, bits):
        keep, send = summed[0], summed[1:]
        if step <= 3 and edges[step] > edges[step - 1]:
            grad = run_head_grad(edges[step - 1], edges[step] - edges[step - 1], normed, dlogits, grad, send)
        if step == 1:
            got = [moved(send[0], 2), moved(send[1], 1)]
        else:
            got = [moved(send[0], 1 << step)]
        cut = keep.shape[1] // 2
        if step < bits - 1 and cut % 16 == 0:
            summed = run_fold((keep,), got, 1, grad)
        else:
            total = keep + (jnp.stack(got) if step == 1 else got[0]).astype(jnp.float32)
            if step < bits - 1:
                summed = [total[:, :cut], pack(total[:, cut:], width)]
            else:
                summed = total
    summed = summed.reshape(tok_dev, -1)
    cross = summed[:, width] + summed[:, width + 1]
    summed = summed[:, :width]

    quarter = tokens // 4
    own = lambda row: jnp.concatenate([row[:half], row[quarter : quarter + half]])
    token_loss = own(table[0]) - own(table[1]) + BETA * cross
    values = own_rows.astype(jnp.float32)
    inverse = lax.rsqrt(jnp.mean(values * values, axis=-1, keepdims=True) + EPS)
    scaled = gain_row * summed
    inner = jnp.mean(scaled * values, axis=-1, keepdims=True)
    hidden_grad = inverse * scaled - values * inverse**3 * inner
    return (token_loss[None], grad.T[None], hidden_grad.astype(jnp.bfloat16)[None])


def solution(mesh):
    in_specs = (P("member", "fsdp", None), P("member", None), P("member", None, "fsdp"), P())
    out_specs = (P("member", "fsdp"), P("member", None, "fsdp"), P("member", "fsdp", None))
    return jax.shard_map(body, mesh=mesh, in_specs=in_specs, out_specs=out_specs, check_vma=False)
```

time: 223 us -> 171 us (0.77)
  waiting for transfers between devices: 91.4 us -> 12.1 us
  Pallas kernels: 86.9 us -> 117 us
  local copies, waits for them, and re-layouts: 5.93 us -> 11.5 us
  other arithmetic: 8 us -> 2.45 us
  starting transfers between devices: 29.2 us -> 26.1 us
    ppermute x19 -> x21, waiting for transfers between devices: 91.4 us -> 12.1 us  [the longest x18 11.4 us: moved(): return lax.ppermute(value, 'fsdp', [(i, i ^ offset) for i in range(n)])]
    pallas_call x3 -> x17, Pallas kernels: 86.9 us -> 117 us  [the longest x2 34.2 us: run_dlogits(): pl.pallas_call(functools.partial(dlogits_kernel, tile, tiles, group), gri...]
    unnamed x13 -> x40, local copies, waits for them, and re-layouts: 0.62 us -> 8.77 us
    ppermute x19 -> x21, starting transfers between devices: 29.2 us -> 26.1 us  [the longest x18 25.5 us: moved(): return lax.ppermute(value, 'fsdp', [(i, i ^ offset) for i in range(n)])]
    slice x12 -> x1, local copies, waits for them, and re-layouts: 3.66 us -> 0.77 us  [body(): own = lambda row: jnp.concatenate([row[:half], row[quarter:quarter + half]])]
    another operation x4 -> x0, other arithmetic: 2.66 us -> none  [gather_blocks(): held = jnp.stack([held, arrived])]
    add x12 -> x2, other arithmetic: 2.96 us -> 0.62 us  [the longest x1 0.59 us: body(): token_loss = own(table[0]) - own(table[1]) + BETA * cross]
  transfers between devices with their start and end apart: 19 -> 21, of which waited for: 14 -> 9; matrix products, arithmetic and copies ran while one was open for 3% -> 2% of each run, Pallas kernels for 10% -> 55%
where the time goes in v2:
time: 171 us; the launch traced here: 170 us
  Pallas kernels  117 us (68%)
  starting transfers between devices  26.1 us (15%)
  waiting for transfers between devices  12.1 us (7%)
  local copies, waits for them, and re-layouts  11.5 us (7%)
  other arithmetic  2.45 us (1%)
    pallas_call x2, Pallas kernels, run_dlogits(): pl.pallas_call(functools.partial(dlogits_kernel, tile, tiles, group), gri...  34.2 us
    pallas_call x2, Pallas kernels, run_logits(): pl.pallas_call(functools.partial(logits_kernel, tile, tiles, group), grid...  33.6 us
    pallas_call x3, Pallas kernels, run_head_grad(): pl.pallas_call(head_grad_kernel, grid=(count,), in_specs=in_specs, out_sp...  28.3 us
    ppermute x18, starting transfers between devices, moved(): return lax.ppermute(value, 'fsdp', [(i, i ^ offset) for i in range(n)])  25.5 us
    pallas_call x2, Pallas kernels, run_load(): pl.pallas_call(functools.partial(load_kernel, first, rows), in_specs=in_s...  11.6 us
    ppermute x18, waiting for transfers between devices, moved(): return lax.ppermute(value, 'fsdp', [(i, i ^ offset) for i in range(n)])  11.4 us
    unnamed x40, local copies, waits for them, and re-layouts  8.77 us
    pallas_call x2, Pallas kernels, run_join(): pl.pallas_call(functools.partial(join_kernel, len(pieces), split), in_spe...  3.55 us
  transfers between devices with their start and end apart: 21, of which 9 were waited for; matrix products, arithmetic and copies ran while one was open for 2% of the time, Pallas kernels for 55%

profile of v2, /device:TPU:0, one launch (start us, length us, event | category | flops | bytes accessed | tf_op | source)
XLA Modules:
  0.0 170.2 jit_solution(8739519729641684176)
XLA Ops:
  0.6 4.1 %collective-permute-start = (bf16[32,2048]{1,0:T(8,128)(2,1)}, bf16[32,2048]{1,0:T(8,128)(2,1)S(1)}, u32[]{:S(2)}, u32[]{:S(2)}) collective-permute-start(bf16[32,2048]{1,0:T(8,128)(2,1)} %bitcast.22), channel_id=1, source_target_pairs={{0,8},{1,9},{2,10},{3,11},{4,12},{5,13},{6,14},{7,15},{8,0},{9,1},... | collective-permute-start | bytes 393224 | tf_op jit(solution)/shard_map/ppermute | solution.py:537
  7.4 5.8 %load.2.refs_2_.refs_1_ = bf16[8016,2048]{1,0:T(8,128)(2,1)S(1)} custom-call(bf16[8016,2048]{1,0:T(8,128)(2,1)} %bitcast.17, s32[1,512]{1,0:T(1,128)} %sub.23.refs_0_.labels_ref), custom_call_target="tpu_custom_call" | custom-call | bytes 32899072 | tf_op jit(solution)/shard_map/load/pallas_call | solution.py:70
  13.9 1.7 join.2.refs_0_
  15.5 1.6 collective-permute-start.1
  17.1 5.8 %load.3.refs_2_.w_ref.refs_3_.refs_4_ = bf16[8016,2048]{1,0:T(8,128)(2,1)S(1)} custom-call(bf16[8016,2048]{1,0:T(8,128)(2,1)} %bitcast.18, bf16[64,2048]{1,0:T(8,128)(2,1)} %join.2.refs_0_, bf16[8016,2048]{1,0:T(8,128)(2,1)S(1)} %load.2.refs_2_.refs_1_), custom_call_target="tpu_custom_call", output_to_operand_aliasing={{}: (2, {})} | custom-call | bytes 32768000 | tf_op jit(solution)/shard_map/load/pallas_call | solution.py:70
  24.2 1.9 %join.3 = (bf16[64,2048]{1,0:T(8,128)(2,1)}, bf16[64,2048]{1,0:T(8,128)(2,1)}) custom-call(bf16[64,2048]{1,0:T(8,128)(2,1)} %join.2.refs_0_, bf16[64,2048]{1,0:T(8,128)(2,1)} %copy-done.10, bf16[8016,2048]{1,0:T(8,128)(2,1)S(1)} %load.3.refs_2_.w_ref.refs_3_.refs_4_), custom_call_target="tpu_custom_call" | custom-call | flops 4096 | bytes 4096 | tf_op jit(solution)/shard_map/join/pallas_call | solution.py:100
  26.1 1.5 collective-permute-start.2
  27.6 1.5 collective-permute-start.3
  29.1 4.1 %collective-permute-done.2.high_a = bf16[64,2048]{1,0:T(8,128)(2,1)S(1)} collective-permute-done((bf16[64,2048]{1,0:T(8,128)(2,1)}, bf16[64,2048]{1,0:T(8,128)(2,1)S(1)}, u32[]{:S(2)}, u32[]{:S(2)}) %collective-permute-start.2) | collective-permute-done | bytes 262176 | tf_op jit(solution)/shard_map/ppermute | solution.py:537
  35.1 2.2 %stack.1 = (bf16[128,2048]{1,0:T(8,128)(2,1)}, bf16[128,2048]{1,0:T(8,128)(2,1)}) custom-call(bf16[8016,2048]{1,0:T(8,128)(2,1)S(1)} %load.3.refs_2_.w_ref.refs_3_.refs_4_, bf16[64,2048]{1,0:T(8,128)(2,1)} %get-tuple-element.30.low_a, bf16[64,2048]{1,0:T(8,128)(2,1)} %copy-done.8, bf16[64,2048]{1,0:T(8,128)(2,1)} %get-tuple-element.31.low_b, ...), custom_call_target="tpu_custom_call" | custom-call | flops 4096 | bytes 4096 | tf_op jit(solution)/shard_map/stack/pallas_call | solution.py:120
  37.3 1.5 collective-permute-start.4
  39.8 16.7 %logits.2 = (bf16[8016,256]{1,0:T(8,128)(2,1)}, bf16[8016,256]{1,0:T(8,128)(2,1)}, bf16[512,2048]{1,0:T(8,128)(2,1)}, f32[8,256]{1,0:T(8,128)}, f32[8,256]{1,0:T(8,128)}) custom-call(bf16[128,2048]{1,0:T(8,128)(2,1)} %get-tuple-element.32.rows_a_ref, bf16[128,2048]{1,0:T(8,128)(2,1)} %get-tuple-element.33.rows_b_ref, f32[1,2048]{1,0:T(1,128)} %gain_ref.3, ...), custom_call_target="tpu_custom_call" | custom-call | flops 8405385216 | bytes 8208384 | tf_op jit(solution)/shard_map/logits/pallas_call | solution.py:282
  57.5 16.9 %logits.3 = (bf16[8016,256]{1,0:T(8,128)(2,1)}, bf16[8016,256]{1,0:T(8,128)(2,1)}, bf16[512,2048]{1,0:T(8,128)(2,1)}, f32[8,512]{1,0:T(8,128)}, f32[8,512]{1,0:T(8,128)}) custom-call(bf16[128,2048]{1,0:T(8,128)(2,1)} %copy-done.6, bf16[128,2048]{1,0:T(8,128)(2,1)} %copy-done.7, f32[1,2048]{1,0:T(1,128)} %gain_ref.3, ...), custom_call_target="tpu_custom_call", output_to_operand_aliasing={{2}: (5, {})} | custom-call | flops 8405385216 | bytes 8208384 | tf_op jit(solution)/shard_map/logits/pallas_call | solution.py:282
  76.9 1.5 collective-permute-start.6
  81.5 1.5 totals.2.table_ref
  83.0 2.5 %collective-permute-start.11 = (f32[8,512]{1,0:T(8,128)}, f32[8,512]{1,0:T(8,128)S(1)}, u32[]{:S(2)}, u32[]{:S(2)}) collective-permute-start(f32[8,512]{1,0:T(8,128)} %totals.2.table_ref), channel_id=1, source_target_pairs={{0,12},{1,13},{2,14},{3,15},{4,8},{5,9},{6,10},{7,11},{8,4},{9,5},... | collective-permute-start | bytes 49160 | tf_op jit(solution)/shard_map/ppermute | solution.py:537
  88.8 1.6 collective-permute-done.10.refs_1_
  91.0 1.6 totals.3.own_ref
  96.0 16.9 %dlogits.2 = (bf16[8016,512]{1,0:T(8,128)(2,1)}, bf16[128,2176]{1,0:T(8,128)(2,1)}, bf16[128,2176]{1,0:T(8,128)(2,1)}) custom-call(f32[16,512]{1,0:T(8,128)} %totals.3.own_ref, f32[16,512]{1,0:T(8,128)} %copy-done.13, s32[1,512]{1,0:T(1,128)} %sub.23.refs_0_.labels_ref, bf16[8016,256]{1,0:T(8,128)(2,1)} %get-tuple-element.41.ps_ref, ...), custom_call_target="tpu_custom_call" | custom-call | flops 8405385216 | bytes 16416768 | tf_op jit(solution)/shard_map/dlogits/pallas_call | solution.py:423
  112.9 1.5 collective-permute-start.15
  115.4 17.4 %dlogits.3 = (bf16[8016,512]{1,0:T(8,128)(2,1)}, f32[128,2176]{1,0:T(8,128)}, f32[128,2176]{1,0:T(8,128)}) custom-call(f32[16,512]{1,0:T(8,128)} %totals.3.own_ref, f32[16,512]{1,0:T(8,128)} %copy-done.13, s32[1,512]{1,0:T(1,128)} %sub.23.refs_0_.labels_ref, bf16[8016,256]{1,0:T(8,128)(2,1)} %get-tuple-element.39.ps_ref, ...), custom_call_target="tpu_custom_call", output_to_operand_aliasing={{0}: (7, {})} | custom-call | flops 8405385216 | bytes 16416768 | tf_op jit(solution)/shard_map/dlogits/pallas_call | solution.py:423
  137.4 10.3 %head_grad.3.refs_3_.refs_1_ = bf16[8016,2048]{1,0:T(8,128)(2,1)} custom-call(bf16[512,2048]{1,0:T(8,128)(2,1)S(1)} %copy-done, bf16[8016,512]{1,0:T(8,128)(2,1)} %get-tuple-element.52.d_ref, bf16[64,2176]{1,0:T(8,128)(2,1)S(1)} %get-tuple-element.49.refs_0_, bf16[64,2176]{1,0:T(8,128)(2,1)S(1)} %get-tuple-element.50.refs_1_), custom_call_target="tpu_custom_call" | custom-call | flops 6442450944 | bytes 15728640 | tf_op jit(solution)/shard_map/head_grad/pallas_call | solution.py:518
  148.9 7.9 %head_grad.4.refs_2_.refs_1_ = bf16[8016,2048]{1,0:T(8,128)(2,1)} custom-call(bf16[512,2048]{1,0:T(8,128)(2,1)S(1)} %copy-done, bf16[8016,512]{1,0:T(8,128)(2,1)} %get-tuple-element.52.d_ref, bf16[2,32,2176]{2,1,0:T(8,128)(2,1)S(1)} %get-tuple-element.54.refs_0_, bf16[8016,2048]{1,0:T(8,128)(2,1)} %head_grad.3.refs_3_.refs_1_), custom_call_target="tpu_custom_call", output_to_operand_aliasing={{}: (3, {})} | custom-call | flops 4294967296 | bytes 10485760 | tf_op jit(solution)/shard_map/head_grad/pallas_call | solution.py:518
  158.4 10.1 %head_grad.5 = bf16[8016,2048]{1,0:T(8,128)(2,1)} custom-call(bf16[512,2048]{1,0:T(8,128)(2,1)S(1)} %copy-done, bf16[8016,512]{1,0:T(8,128)(2,1)} %get-tuple-element.52.d_ref, bf16[2,16,2176]{2,1,0:T(8,128)(2,1)S(1)} %get-tuple-element.56.refs_0_, bf16[8016,2048]{1,0:T(8,128)(2,1)} %head_grad.4.refs_2_.refs_1_), custom_call_target="tpu_custom_call", output_to_operand_aliasing={{}: (3, {})} | custom-call | flops 6442450944 | bytes 15728640 | tf_op jit(solution)/shard_map/head_grad/pallas_call | solution.py:518
  (88 shorter events, 31.4 us)
Async XLA Ops:
  0.6 12.6 %collective-permute-start = (bf16[32,2048]{1,0:T(8,128)(2,1)}, bf16[32,2048]{1,0:T(8,128)(2,1)S(1)}, u32[]{:S(2)}, u32[]{:S(2)}) collective-permute-start(bf16[32,2048]{1,0:T(8,128)(2,1)} %bitcast.22), channel_id=1, source_target_pairs={{0,8},{1,9},{2,10},{3,11},{4,12},{5,13},{6,14},{7,15},{8,0},{9,1},... | collective-permute-start | bytes 393224 | tf_op jit(solution)/shard_map/ppermute | solution.py:537
  15.5 8.0 %collective-permute-start.1 = (bf16[64,2048]{1,0:T(8,128)(2,1)}, bf16[64,2048]{1,0:T(8,128)(2,1)S(1)}, u32[]{:S(2)}, u32[]{:S(2)}) collective-permute-start(bf16[64,2048]{1,0:T(8,128)(2,1)} %join.2.refs_0_), channel_id=1, source_target_pairs={{0,4},{1,5},{2,6},{3,7},{4,0},{5,1},{6,2},{7,3},{8,12},{9,13},{10,... | collective-permute-start | bytes 786440 | tf_op jit(solution)/shard_map/ppermute | solution.py:537
  26.1 7.1 %collective-permute-start.2 = (bf16[64,2048]{1,0:T(8,128)(2,1)}, bf16[64,2048]{1,0:T(8,128)(2,1)S(1)}, u32[]{:S(2)}, u32[]{:S(2)}) collective-permute-start(bf16[64,2048]{1,0:T(8,128)(2,1)} %get-tuple-element.30.low_a), channel_id=1, source_target_pairs={{0,2},{1,3},{2,0},{3,1},{4,6},{5,7},{6,4},{7,5},{8,10},{9,11},{10,... | collective-permute-start | bytes 786440 | tf_op jit(solution)/shard_map/ppermute | solution.py:537
  27.6 6.8 %collective-permute-start.3 = (bf16[64,2048]{1,0:T(8,128)(2,1)}, bf16[64,2048]{1,0:T(8,128)(2,1)S(1)}, u32[]{:S(2)}, u32[]{:S(2)}) collective-permute-start(bf16[64,2048]{1,0:T(8,128)(2,1)} %get-tuple-element.31.low_b), channel_id=1, source_target_pairs={{0,1},{1,0},{2,3},{3,2},{4,5},{5,4},{6,7},{7,6},{8,9},{9,8},{10,11... | collective-permute-start | bytes 786440 | tf_op jit(solution)/shard_map/ppermute | solution.py:537
  37.3 19.2 %collective-permute-start.4 = (bf16[128,2048]{1,0:T(8,128)(2,1)}, bf16[128,2048]{1,0:T(8,128)(2,1)S(1)}, u32[]{:S(2)}, u32[]{:S(2)}) collective-permute-start(bf16[128,2048]{1,0:T(8,128)(2,1)} %get-tuple-element.32.rows_a_ref), channel_id=1, source_target_pairs={{0,1},{1,0},{2,3},{3,2},{4,5},{5,4},{6,7},{7,6},{8,9},{9,8},{10,11... | collective-permute-start | bytes 1572872 | tf_op jit(solution)/shard_map/ppermute | solution.py:537
  38.8 17.7 %collective-permute-start.5 = (bf16[128,2048]{1,0:T(8,128)(2,1)}, bf16[128,2048]{1,0:T(8,128)(2,1)S(1)}, u32[]{:S(2)}, u32[]{:S(2)}) collective-permute-start(bf16[128,2048]{1,0:T(8,128)(2,1)} %get-tuple-element.33.rows_b_ref), channel_id=1, source_target_pairs={{0,2},{1,3},{2,0},{3,1},{4,6},{5,7},{6,4},{7,5},{8,10},{9,11},{10,... | collective-permute-start | bytes 1572872 | tf_op jit(solution)/shard_map/ppermute | solution.py:537
  57.5 16.9 %copy-start.3 = (bf16[8016,256]{1,0:T(8,128)(2,1)S(1)}, bf16[8016,256]{1,0:T(8,128)(2,1)}, u32[]{:S(2)}) copy-start(bf16[8016,256]{1,0:T(8,128)(2,1)} %get-tuple-element.39.ps_ref) | copy-start | bytes 12312580
  74.3 19.7 %collective-permute-start.14 = (bf16[8016,256]{1,0:T(8,128)(2,1)}, bf16[8016,256]{1,0:T(8,128)(2,1)S(1)}, u32[]{:S(2)}, u32[]{:S(2)}) collective-permute-start(bf16[8016,256]{1,0:T(8,128)(2,1)} %get-tuple-element.41.ps_ref), channel_id=1, source_target_pairs={{0,16},{16,0},{1,17},{17,1},{2,18},{18,2},{3,19},{19,3},{4,20},{20... | collective-permute-start | bytes 12312584 | tf_op jit(solution)/shard_map/ppermute | solution.py:541
  74.4 41.0 %collective-permute-start.13 = (bf16[8016,256]{1,0:T(8,128)(2,1)S(1)}, bf16[8016,256]{1,0:T(8,128)(2,1)}, u32[]{:S(2)}, u32[]{:S(2)}) collective-permute-start(bf16[8016,256]{1,0:T(8,128)(2,1)S(1)} %copy-done.3), channel_id=1, source_target_pairs={{0,16},{16,0},{1,17},{17,1},{2,18},{18,2},{3,19},{19,3},{4,20},{20... | collective-permute-start | bytes 12312584 | tf_op jit(solution)/shard_map/ppermute | solution.py:541
  74.9 4.9 %collective-permute-start.8 = (f32[8,512]{1,0:T(8,128)}, f32[8,512]{1,0:T(8,128)S(1)}, u32[]{:S(2)}, u32[]{:S(2)}) collective-permute-start(f32[8,512]{1,0:T(8,128)} %get-tuple-element.37.table_ref), channel_id=1, source_target_pairs={{0,3},{1,2},{2,1},{3,0},{4,7},{5,6},{6,5},{7,4},{8,11},{9,10},{10,... | collective-permute-start | bytes 49160 | tf_op jit(solution)/shard_map/ppermute | solution.py:537
  75.9 4.0 %collective-permute-start.7 = (f32[8,512]{1,0:T(8,128)}, f32[8,512]{1,0:T(8,128)S(1)}, u32[]{:S(2)}, u32[]{:S(2)}) collective-permute-start(f32[8,512]{1,0:T(8,128)} %get-tuple-element.37.table_ref), channel_id=1, source_target_pairs={{0,2},{1,3},{2,0},{3,1},{4,6},{5,7},{6,4},{7,5},{8,10},{9,11},{10,... | collective-permute-start | bytes 49160 | tf_op jit(solution)/shard_map/ppermute | solution.py:537
  76.9 3.9 %collective-permute-start.6 = (f32[8,512]{1,0:T(8,128)}, f32[8,512]{1,0:T(8,128)S(1)}, u32[]{:S(2)}, u32[]{:S(2)}) collective-permute-start(f32[8,512]{1,0:T(8,128)} %get-tuple-element.37.table_ref), channel_id=1, source_target_pairs={{0,1},{1,0},{2,3},{3,2},{4,5},{5,4},{6,7},{7,6},{8,9},{9,8},{10,11... | collective-permute-start | bytes 49160 | tf_op jit(solution)/shard_map/ppermute | solution.py:537
  83.0 5.7 %collective-permute-start.11 = (f32[8,512]{1,0:T(8,128)}, f32[8,512]{1,0:T(8,128)S(1)}, u32[]{:S(2)}, u32[]{:S(2)}) collective-permute-start(f32[8,512]{1,0:T(8,128)} %totals.2.table_ref), channel_id=1, source_target_pairs={{0,12},{1,13},{2,14},{3,15},{4,8},{5,9},{6,10},{7,11},{8,4},{9,5},... | collective-permute-start | bytes 49160 | tf_op jit(solution)/shard_map/ppermute | solution.py:537
  85.6 4.8 %collective-permute-start.10 = (f32[8,512]{1,0:T(8,128)}, f32[8,512]{1,0:T(8,128)S(1)}, u32[]{:S(2)}, u32[]{:S(2)}) collective-permute-start(f32[8,512]{1,0:T(8,128)} %totals.2.table_ref), channel_id=1, source_target_pairs={{0,8},{1,9},{2,10},{3,11},{4,12},{5,13},{6,14},{7,15},{8,0},{9,1},... | collective-permute-start | bytes 49160 | tf_op jit(solution)/shard_map/ppermute | solution.py:537
  86.0 4.4 %collective-permute-start.9 = (f32[8,512]{1,0:T(8,128)}, f32[8,512]{1,0:T(8,128)S(1)}, u32[]{:S(2)}, u32[]{:S(2)}) collective-permute-start(f32[8,512]{1,0:T(8,128)} %totals.2.table_ref), channel_id=1, source_target_pairs={{0,4},{1,5},{2,6},{3,7},{4,0},{5,1},{6,2},{7,3},{8,12},{9,13},{10,... | collective-permute-start | bytes 49160 | tf_op jit(solution)/shard_map/ppermute | solution.py:537
  92.6 1.4 collective-permute-start.12
  112.9 19.9 %collective-permute-start.15 = (bf16[128,2176]{1,0:T(8,128)(2,1)}, bf16[128,2176]{1,0:T(8,128)(2,1)S(1)}, u32[]{:S(2)}, u32[]{:S(2)}) collective-permute-start(bf16[128,2176]{1,0:T(8,128)(2,1)} %get-tuple-element.46), channel_id=1, source_target_pairs={{0,1},{1,0},{2,3},{3,2},{4,5},{5,4},{6,7},{7,6},{8,9},{9,8},{10,11... | collective-permute-start | bytes 1671176 | tf_op jit(solution)/shard_map/ppermute | solution.py:537
  114.3 18.4 %collective-permute-start.16 = (bf16[128,2176]{1,0:T(8,128)(2,1)}, bf16[128,2176]{1,0:T(8,128)(2,1)S(1)}, u32[]{:S(2)}, u32[]{:S(2)}) collective-permute-start(bf16[128,2176]{1,0:T(8,128)(2,1)} %get-tuple-element.47), channel_id=1, source_target_pairs={{0,2},{1,3},{2,0},{3,1},{4,6},{5,7},{6,4},{7,5},{8,10},{9,11},{10,... | collective-permute-start | bytes 1671176 | tf_op jit(solution)/shard_map/ppermute | solution.py:537
  135.8 11.9 %collective-permute-start.17 = (bf16[64,2176]{1,0:T(8,128)(2,1)S(1)}, bf16[64,2176]{1,0:T(8,128)(2,1)S(1)}, u32[]{:S(2)}, u32[]{:S(2)}) collective-permute-start(bf16[64,2176]{1,0:T(8,128)(2,1)S(1)} %get-tuple-element.49.refs_0_), channel_id=1, source_target_pairs={{0,2},{1,3},{2,0},{3,1},{4,6},{5,7},{6,4},{7,5},{8,10},{9,11},{10,... | collective-permute-start | bytes 835592 | tf_op jit(solution)/shard_map/ppermute | solution.py:537
  136.8 10.9 %collective-permute-start.18 = (bf16[64,2176]{1,0:T(8,128)(2,1)S(1)}, bf16[64,2176]{1,0:T(8,128)(2,1)S(1)}, u32[]{:S(2)}, u32[]{:S(2)}) collective-permute-start(bf16[64,2176]{1,0:T(8,128)(2,1)S(1)} %get-tuple-element.50.refs_1_), channel_id=1, source_target_pairs={{0,1},{1,0},{2,3},{3,2},{4,5},{5,4},{6,7},{7,6},{8,9},{9,8},{10,11... | collective-permute-start | bytes 835592 | tf_op jit(solution)/shard_map/ppermute | solution.py:537
  147.9 8.9 %collective-permute-start.19 = (bf16[2,32,2176]{2,1,0:T(8,128)(2,1)S(1)}, bf16[2,32,2176]{2,1,0:T(8,128)(2,1)S(1)}, u32[]{:S(2)}, u32[]{:S(2)}) collective-permute-start(bf16[2,32,2176]{2,1,0:T(8,128)(2,1)S(1)} %get-tuple-element.54.refs_0_), channel_id=1, source_target_pairs={{0,4},{1,5},{2,6},{3,7},{4,0},{5,1},{6,2},{7,3},{8,12},{9,13},{10,... | collective-permute-start | bytes 835592 | tf_op jit(solution)/shard_map/ppermute | solution.py:537
  157.0 11.7 %copy-start.5 = (bf16[1,32,2048]{2,1,0:T(8,128)(2,1)S(1)}, bf16[1,32,2048]{2,1,0:T(8,128)(2,1)}, u32[]{:S(2)}) copy-start(bf16[1,32,2048]{2,1,0:T(8,128)(2,1)} %param.6) | copy-start | bytes 393220
  157.0 11.7 %copy-start.12 = (f32[1,2048]{1,0:T(1,128)S(1)}, f32[1,2048]{1,0:T(1,128)}, u32[]{:S(2)}) copy-start(f32[1,2048]{1,0:T(1,128)} %gain_ref.3) | copy-start | bytes 24580
  157.0 11.5 %collective-permute-start.20 = (bf16[2,16,2176]{2,1,0:T(8,128)(2,1)S(1)}, bf16[2,16,2176]{2,1,0:T(8,128)(2,1)S(1)}, u32[]{:S(2)}, u32[]{:S(2)}) collective-permute-start(bf16[2,16,2176]{2,1,0:T(8,128)(2,1)S(1)} %get-tuple-element.56.refs_0_), channel_id=1, source_target_pairs={{0,8},{1,9},{2,10},{3,11},{4,12},{5,13},{6,14},{7,15},{8,0},{9,1},... | collective-permute-start | bytes 417800 | tf_op jit(solution)/shard_map/ppermute | solution.py:537
  (17 other events, 20.3 us)

commit v3 on v2

--- a/solution.py
+++ b/solution.py
@@ -9,9 +9,11 @@
 EPS = 1e-05
 BETA = 0.5
 TILE = 1024
+GRAD_TILE = 1024
 CHUNK = 128
+PIECE = 512
 LANES = 128
-VMEM_SHARED = 24 * 1024 * 1024
+VMEM_SHARED = 34200000
 VMEM_ALONE = 40 * 1024 * 1024
 GRAD_EDGES = (0, 3, 5, 8)
 LOAD_COPIES = 4
@@ -22,8 +24,8 @@
     return -(-a // b)
 
 
-def tiling(vocab_dev):
-    tile = min(TILE, vocab_dev)
+def tiling(vocab_dev, tile):
+    tile = min(tile, vocab_dev)
     return tile, cdiv(vocab_dev, tile)
 
 
@@ -33,6 +35,19 @@
 
 def whole_vmem():
     return pl.BlockSpec(memory_space=pltpu.VMEM)
+
+
+def together(first, second):
+    done = 0
+    for i, work in enumerate(first):
+        work()
+        upto = len(second) * (i + 1) // len(first)
+        for other in second[done:upto]:
+            other()
+        done = upto
+    if not first:
+        for other in second:
+            other()
 
 
 def pinned(value):
@@ -178,42 +193,60 @@
 def logits_kernel(
     tile, tiles, group_index, rows_a_ref, rows_b_ref, gain_ref, labels_ref, w_ref, *refs
 ):
-    p_ref, l_ref, normed_ref, tops_ref, stats_ref, logits_ref, m_ref, s_ref, picked_ref = refs[-9:]
+    p_ref, l_ref, normed_ref, tops_ref, stats_ref, even_ref, odd_ref, m_ref, s_ref, picked_ref = refs[-10:]
+    logits_refs = even_ref, odd_ref
     step = pl.program_id(0)
     tokens = normed_ref.shape[0]
     last_rows = w_ref.shape[0] - (tiles - 1) * tile
 
     def matmul(slot, start, rows):
-        logits_ref[slot, :rows, :] = lax.dot_general(
-            w_ref[pl.ds(start, rows), :], normed_ref[...], (((1,), (1,)), ((), ())),
-            preferred_element_type=jnp.float32,
-        )
+        def piece(place, size):
+            def work():
+                logits_refs[slot][place : place + size, :] = lax.dot_general(
+                    w_ref[pl.ds(start + place, size), :], normed_ref[...], (((1,), (1,)), ((), ())),
+                    preferred_element_type=jnp.float32,
+                )
+
+            return work
+
+        return [piece(place, min(PIECE, rows - place)) for place in range(0, rows, PIECE)]
 
     def soften(slot, index, valid_rows):
         group = min(tokens, LANES)
+        items = []
         for col in range(0, tokens, group):
+            state = {}
             cols = slice(col, col + group)
             target = labels_ref[:, group_index * tokens + col : group_index * tokens + col + group] - index * tile
-            top = None
-            for start, rows in chunks(valid_rows):
-                part = jnp.max(logits_ref[slot, start : start + rows, cols], axis=0, keepdims=True)
-                top = part if top is None else jnp.maximum(top, part)
-            total = jnp.zeros((1, group), jnp.float32)
-            picked = picked_ref[:, cols]
-            for start, rows in chunks(valid_rows):
-                values = logits_ref[slot, start : start + rows, cols]
+
+            def find_top(cols=cols, state=state):
+                top = None
+                for start, rows in chunks(valid_rows):
+                    part = jnp.max(logits_refs[slot][start : start + rows, cols], axis=0, keepdims=True)
+                    top = part if top is None else jnp.maximum(top, part)
+                state.update(top=top, total=jnp.zeros((1, group), jnp.float32), picked=picked_ref[:, cols])
+
+            def chunk(start, rows, cols=cols, state=state, target=target):
+                values = logits_refs[slot][start : start + rows, cols]
                 row = lax.broadcasted_iota(jnp.int32, (rows, group), 0)
-                lowered = values - top
+                lowered = values - state["top"]
                 exps = jnp.exp(lowered)
                 l_ref[start : start + rows, cols] = lowered.astype(l_ref.dtype)
                 p_ref[start : start + rows, cols] = exps.astype(p_ref.dtype)
                 chosen = jnp.where(row == target - start, values, 0.0)
-                total = total + jnp.sum(exps, axis=0, keepdims=True)
-                picked = picked + jnp.sum(chosen, axis=0, keepdims=True)
-            here = lax.broadcasted_iota(jnp.int32, (m_ref.shape[0], group), 0) == index
-            m_ref[:, cols] = jnp.where(here, top, m_ref[:, cols])
-            s_ref[:, cols] = jnp.where(here, total, s_ref[:, cols])
-            picked_ref[:, cols] = picked
+                state["total"] = state["total"] + jnp.sum(exps, axis=0, keepdims=True)
+                state["picked"] = state["picked"] + jnp.sum(chosen, axis=0, keepdims=True)
+
+            def finish(cols=cols, state=state):
+                here = lax.broadcasted_iota(jnp.int32, (m_ref.shape[0], group), 0) == index
+                m_ref[:, cols] = jnp.where(here, state["top"], m_ref[:, cols])
+                s_ref[:, cols] = jnp.where(here, state["total"], s_ref[:, cols])
+                picked_ref[:, cols] = state["picked"]
+
+            items.append(find_top)
+            items += [functools.partial(chunk, start, rows) for start, rows in chunks(valid_rows)]
+            items.append(finish)
+        return items
 
     @pl.when(step == 0)
     def _():
@@ -225,25 +258,25 @@
         m_ref[...] = jnp.full_like(m_ref, -jnp.inf)
         s_ref[...] = jnp.zeros_like(s_ref)
         picked_ref[...] = jnp.zeros_like(picked_ref)
-        matmul(0, 0, last_rows if tiles == 1 else tile)
+        together(matmul(0, 0, last_rows if tiles == 1 else tile), [])
 
     if tiles > 2:
 
-        @pl.when((step > 0) & (step < tiles - 1))
-        def _():
-            matmul(lax.rem(step, 2), pl.multiple_of(step * tile, tile), tile)
-            soften(lax.rem(step + 1, 2), step - 1, tile)
+        for parity in range(2):
+
+            @pl.when((step > 0) & (step < tiles - 1) & (lax.rem(step, 2) == parity))
+            def _(parity=parity):
+                together(matmul(parity, pl.multiple_of(step * tile, tile), tile), soften(1 - parity, step - 1, tile))
 
     if tiles > 1:
 
         @pl.when(step == tiles - 1)
         def _():
-            matmul((tiles - 1) % 2, (tiles - 1) * tile, last_rows)
-            soften(tiles % 2, tiles - 2, tile)
+            together(matmul((tiles - 1) % 2, (tiles - 1) * tile, last_rows), soften(tiles % 2, tiles - 2, tile))
 
     @pl.when(step == tiles)
     def _():
-        soften((tiles - 1) % 2, tiles - 1, last_rows)
+        together([], soften((tiles - 1) % 2, tiles - 1, last_rows))
         tops = m_ref[...]
         top = jnp.max(tops, axis=0, keepdims=True)
         total = jnp.sum(s_ref[...] * jnp.exp(tops - top), axis=0, keepdims=True)
@@ -263,7 +296,7 @@
     half, width = rows_a.shape
     tokens = 2 * half
     vocab_dev = weights.shape[0]
-    tile, tiles = tiling(vocab_dev)
+    tile, tiles = tiling(vocab_dev, TILE)
     groups = cdiv(tiles, 8) * 8
     behind = pl.BlockSpec((tile, tokens), lambda j: (jnp.maximum(j - 1, 0), 0))
     operands = [rows_a, rows_b, gain, labels, weights]
@@ -298,7 +331,8 @@
             jax.ShapeDtypeStruct((8, (group + 1) * tokens), jnp.float32),
         ],
         scratch_shapes=[
-            pltpu.VMEM((2, tile, tokens), jnp.float32),
+            pltpu.VMEM((tile, tokens), jnp.float32),
+            pltpu.VMEM((tile, tokens), jnp.float32),
             pltpu.VMEM((groups, tokens), jnp.float32),
             pltpu.VMEM((groups, tokens), jnp.float32),
             pltpu.VMEM((1, tokens), jnp.float32),
@@ -317,7 +351,8 @@
 def dlogits_kernel(
     tile, tiles, group_index, own_ref, other_ref, labels_ref, ps_ref, pt_ref, l_ref, w_ref, *refs
 ):
-    d_ref, first_ref, second_ref, up_ref, d_scratch, a_ref, b_ref, g_ref, c_ref = refs[-9:]
+    d_ref, first_ref, second_ref, up_ref, even_ref, odd_ref, a_ref, b_ref, g_ref, c_ref = refs[-10:]
+    d_refs = even_ref, odd_ref
     step = pl.program_id(0)
     tokens = ps_ref.shape[1]
     all_tokens = labels_ref.shape[1]
@@ -327,32 +362,53 @@
 
     def weigh(slot, index, valid_rows):
         group = min(tokens, LANES)
+        items = []
         for col in range(0, tokens, group):
+            state = {}
             cols = slice(col, col + group)
             target = labels_ref[:, first + col : first + col + group] - index * tile
-            own, other, gap = (pick_row(ref[:, cols], index) for ref in (a_ref, b_ref, g_ref))
-            cross = c_ref[:, cols]
-            for start, rows in chunks(valid_rows):
+
+            def begin(cols=cols, state=state):
+                state.update(
+                    own=pick_row(a_ref[:, cols], index),
+                    other=pick_row(b_ref[:, cols], index),
+                    gap=pick_row(g_ref[:, cols], index),
+                    cross=c_ref[:, cols],
+                )
+
+            def chunk(start, rows, cols=cols, state=state, target=target):
                 here = slice(start, start + rows)
                 row = lax.broadcasted_iota(jnp.int32, (rows, group), 0)
-                student = ps_ref[here, cols].astype(jnp.float32) * own
-                teacher = pt_ref[here, cols].astype(jnp.float32) * other
+                student = ps_ref[here, cols].astype(jnp.float32) * state["own"]
+                teacher = pt_ref[here, cols].astype(jnp.float32) * state["other"]
                 lowered = l_ref[here, cols].astype(jnp.float32)
-                part = teacher * (gap - lowered)
+                part = teacher * (state["gap"] - lowered)
                 value = student - teacher - jnp.where(row == target - start, scale, 0.0)
-                cross = cross + jnp.sum(part, axis=0, keepdims=True)
+                state["cross"] = state["cross"] + jnp.sum(part, axis=0, keepdims=True)
                 value = value.astype(jnp.bfloat16)
                 d_ref[here, cols] = value
-                d_scratch[slot, here, cols] = value
-            c_ref[:, cols] = cross
+                d_refs[slot][here, cols] = value
+
+            def finish(cols=cols, state=state):
+                c_ref[:, cols] = state["cross"]
+
+            items.append(begin)
+            items += [functools.partial(chunk, start, rows) for start, rows in chunks(valid_rows)]
+            items.append(finish)
+        return items
 
     def matmul(slot, start, rows):
-        for out in range(0, up_ref.shape[1], 512):
-            cols = slice(out, out + 512)
-            up_ref[:, cols] += lax.dot_general(
-                d_scratch[slot, :rows, :], w_ref[pl.ds(start, rows), cols], (((0,), (0,)), ((), ())),
-                preferred_element_type=jnp.float32,
-            )
+        def piece(out):
+            def work():
+                cols = slice(out, out + PIECE)
+                up_ref[:, cols] += lax.dot_general(
+                    d_refs[slot][:rows, :], w_ref[pl.ds(start, rows), cols], (((0,), (0,)), ((), ())),
+                    preferred_element_type=jnp.float32,
+                )
+
+            return work
+
+        return [piece(out) for out in range(0, up_ref.shape[1], PIECE)]
 
     @pl.when(step == 0)
     def _():
@@ -363,25 +419,25 @@
         g_ref[...] = own_total - own_ref[8:, here]
         c_ref[...] = jnp.zeros_like(c_ref)
         up_ref[...] = jnp.zeros_like(up_ref)
-        weigh(0, 0, last_rows if tiles == 1 else tile)
+        together([], weigh(0, 0, last_rows if tiles == 1 else tile))
 
     if tiles > 2:
 
-        @pl.when((step > 0) & (step < tiles - 1))
-        def _():
-            matmul(lax.rem(step + 1, 2), pl.multiple_of((step - 1) * tile, tile), tile)
-            weigh(lax.rem(step, 2), step, tile)
+        for parity in range(2):
+
+            @pl.when((step > 0) & (step < tiles - 1) & (lax.rem(step, 2) == parity))
+            def _(parity=parity):
+                together(matmul(1 - parity, pl.multiple_of((step - 1) * tile, tile), tile), weigh(parity, step, tile))
 
     if tiles > 1:
 
         @pl.when(step == tiles - 1)
         def _():
-            matmul(tiles % 2, (tiles - 2) * tile, tile)
-            weigh((tiles - 1) % 2, tiles - 1, last_rows)
+            together(matmul(tiles % 2, (tiles - 2) * tile, tile), weigh((tiles - 1) % 2, tiles - 1, last_rows))
 
     @pl.when(step == tiles)
     def _():
-        matmul((tiles - 1) % 2, (tiles - 1) * tile, last_rows)
+        together(matmul((tiles - 1) % 2, (tiles - 1) * tile, last_rows), [])
         width = up_ref.shape[1]
         half = tokens // 2
         column = jnp.broadcast_to(c_ref[...] * (all_tokens / BETA), (LANES, tokens)).T
@@ -399,7 +455,7 @@
 def run_dlogits(group, totals, other_totals, labels, p_own, p_other, lowered, weights, dlogits, out_type):
     tokens = p_own.shape[1]
     vocab_dev, width = weights.shape
-    tile, tiles = tiling(vocab_dev)
+    tile, tiles = tiling(vocab_dev, TILE)
     groups = totals.shape[0] - 8
     wide = width + LANES
     ahead = lambda j: jnp.minimum(j, tiles - 1)
@@ -436,7 +492,8 @@
         ],
         scratch_shapes=[
             pltpu.VMEM((tokens, width), jnp.float32),
-            pltpu.VMEM((2, tile, tokens), jnp.bfloat16),
+            pltpu.VMEM((tile, tokens), jnp.bfloat16),
+            pltpu.VMEM((tile, tokens), jnp.bfloat16),
             pltpu.VMEM((groups, tokens), jnp.float32),
             pltpu.VMEM((groups, tokens), jnp.float32),
             pltpu.VMEM((groups, tokens), jnp.float32),
@@ -504,7 +561,7 @@
 def run_head_grad(first, count, normed, dlogits, grad, after):
     tokens, width = normed.shape
     vocab_dev = dlogits.shape[0]
-    tile, tiles = tiling(vocab_dev)
+    tile, tiles = tiling(vocab_dev, GRAD_TILE)
     operands = [normed, pltpu.with_memory_space_constraint(dlogits, pltpu.HBM)]
     in_specs = [whole((tokens, width)), pl.BlockSpec((tile, tokens), lambda j: (first + j, 0))]
     aliases = {}
@@ -622,7 +679,7 @@
         0, table, other_totals, local_labels, p_near, p_near_other, l_near, weights, dlogits, jnp.float32
     )
 
-    tile, tiles = tiling(vocab_dev)
+    tile, tiles = tiling(vocab_dev, GRAD_TILE)
     edges = [tiles * i // 8 for i in GRAD_EDGES]
     grad = None
     summed, sends = run_fold((sum_a, sum_b), (got_a, got_b), 2, None), 2

time: 171 us -> 163 us (0.953)
  local copies, waits for them, and re-layouts: 11.5 us -> 5.94 us
  Pallas kernels: 117 us -> 115 us
    unnamed x40 -> x14, local copies, waits for them, and re-layouts: 8.77 us -> 2.65 us
    pallas_call x2, Pallas kernels: 34.2 us -> 32.2 us  [run_dlogits(): pl.pallas_call(functools.partial(dlogits_kernel, tile, tiles, group), gri...]
  transfers between devices with their start and end apart: 21 -> 21, of which waited for: 9 -> 9; matrix products, arithmetic and copies ran while one was open for 2% -> 2% of each run, Pallas kernels for 55% -> 56%
where the time goes in v3:
time: 163 us; the launch traced here: 162 us
  Pallas kernels  115 us (71%)
  starting transfers between devices  25.4 us (16%)
  waiting for transfers between devices  12.2 us (7%)
  local copies, waits for them, and re-layouts  5.94 us (4%)
  other arithmetic  2.45 us (2%)
    pallas_call x2, Pallas kernels, run_dlogits(): pl.pallas_call(functools.partial(dlogits_kernel, tile, tiles, group), gri...  32.2 us
    pallas_call x2, Pallas kernels, run_logits(): pl.pallas_call(functools.partial(logits_kernel, tile, tiles, group), grid...  32.1 us
    pallas_call x3, Pallas kernels, run_head_grad(): pl.pallas_call(head_grad_kernel, grid=(count,), in_specs=in_specs, out_sp...  28.3 us
    ppermute x18, starting transfers between devices, moved(): return lax.ppermute(value, 'fsdp', [(i, i ^ offset) for i in range(n)])  24.8 us
    ppermute x18, waiting for transfers between devices, moved(): return lax.ppermute(value, 'fsdp', [(i, i ^ offset) for i in range(n)])  11.9 us
    pallas_call x2, Pallas kernels, run_load(): pl.pallas_call(functools.partial(load_kernel, first, rows), in_specs=in_s...  11.6 us
    pallas_call x2, Pallas kernels, run_join(): pl.pallas_call(functools.partial(join_kernel, len(pieces), split), in_spe...  3.56 us
  transfers between devices with their start and end apart: 21, of which 9 were waited for; matrix products, arithmetic and copies ran while one was open for 2% of the time, Pallas kernels for 56%

profile of v3, /device:TPU:0, one launch (start us, length us, event | category | flops | bytes accessed | tf_op | source)
XLA Modules:
  0.0 161.9 jit_solution(12434117553628945492)
XLA Ops:
  0.6 4.1 %collective-permute-start = (bf16[32,2048]{1,0:T(8,128)(2,1)}, bf16[32,2048]{1,0:T(8,128)(2,1)}, u32[]{:S(2)}, u32[]{:S(2)}) collective-permute-start(bf16[32,2048]{1,0:T(8,128)(2,1)} %bitcast.22), channel_id=1, source_target_pairs={{0,8},{1,9},{2,10},{3,11},{4,12},{5,13},{6,14},{7,15},{8,0},{9,1},... | collective-permute-start | bytes 393224 | tf_op jit(solution)/shard_map/ppermute | solution.py:594
  7.4 5.8 %load.2.refs_2_.refs_1_ = bf16[8016,2048]{1,0:T(8,128)(2,1)S(1)} custom-call(bf16[8016,2048]{1,0:T(8,128)(2,1)} %bitcast.17, s32[1,512]{1,0:T(1,128)} %sub.23.refs_0_.labels_ref), custom_call_target="tpu_custom_call" | custom-call | bytes 32899072 | tf_op jit(solution)/shard_map/load/pallas_call | solution.py:85
  13.3 1.7 %join.2.refs_0_ = bf16[64,2048]{1,0:T(8,128)(2,1)} custom-call(bf16[32,2048]{1,0:T(8,128)(2,1)} %bitcast.23, bf16[32,2048]{1,0:T(8,128)(2,1)} %collective-permute-done.refs_1_, bf16[8016,2048]{1,0:T(8,128)(2,1)S(1)} %load.2.refs_2_.refs_1_), custom_call_target="tpu_custom_call" | custom-call | flops 4096 | bytes 4096 | tf_op jit(solution)/shard_map/join/pallas_call | solution.py:115
  14.9 1.6 collective-permute-start.1
  16.5 5.8 %load.3.refs_2_.w_ref.refs_3_.refs_4_ = bf16[8016,2048]{1,0:T(8,128)(2,1)S(1)} custom-call(bf16[8016,2048]{1,0:T(8,128)(2,1)} %bitcast.18, bf16[64,2048]{1,0:T(8,128)(2,1)} %join.2.refs_0_, bf16[8016,2048]{1,0:T(8,128)(2,1)S(1)} %load.2.refs_2_.refs_1_), custom_call_target="tpu_custom_call", output_to_operand_aliasing={{}: (2, {})} | custom-call | bytes 32768000 | tf_op jit(solution)/shard_map/load/pallas_call | solution.py:85
  23.0 1.9 %join.3 = (bf16[64,2048]{1,0:T(8,128)(2,1)}, bf16[64,2048]{1,0:T(8,128)(2,1)}) custom-call(bf16[64,2048]{1,0:T(8,128)(2,1)} %join.2.refs_0_, bf16[64,2048]{1,0:T(8,128)(2,1)} %collective-permute-done.1.refs_1_, bf16[8016,2048]{1,0:T(8,128)(2,1)S(1)} %load.3.refs_2_.w_ref.refs_3_.refs_4_), custom_call_target="tpu_custom_call" | custom-call | flops 4096 | bytes 4096 | tf_op jit(solution)/shard_map/join/pallas_call | solution.py:115
  24.9 1.5 collective-permute-start.2
  27.9 4.2 %collective-permute-done.2.high_a = bf16[64,2048]{1,0:T(8,128)(2,1)} collective-permute-done((bf16[64,2048]{1,0:T(8,128)(2,1)}, bf16[64,2048]{1,0:T(8,128)(2,1)}, u32[]{:S(2)}, u32[]{:S(2)}) %collective-permute-start.2) | collective-permute-done | bytes 262176 | tf_op jit(solution)/shard_map/ppermute | solution.py:594
  33.3 2.2 %stack.1 = (bf16[128,2048]{1,0:T(8,128)(2,1)}, bf16[128,2048]{1,0:T(8,128)(2,1)}) custom-call(bf16[8016,2048]{1,0:T(8,128)(2,1)S(1)} %load.3.refs_2_.w_ref.refs_3_.refs_4_, bf16[64,2048]{1,0:T(8,128)(2,1)} %get-tuple-element.30.low_a, bf16[64,2048]{1,0:T(8,128)(2,1)} %collective-permute-done.2.high_a, bf16[64,2048]{1,0:T(8,128)(2,1)} %get-tuple-element.31.low_b, ...), custom_call_target="tpu_custom_call" | custom-call | flops 4096 | bytes 4096 | tf_op jit(solution)/shard_map/stack/pallas_call | solution.py:135
  37.5 16.0 %logits.2 = (bf16[8016,256]{1,0:T(8,128)(2,1)}, bf16[8016,256]{1,0:T(8,128)(2,1)}, bf16[512,2048]{1,0:T(8,128)(2,1)}, f32[8,256]{1,0:T(8,128)}, f32[8,256]{1,0:T(8,128)}) custom-call(bf16[128,2048]{1,0:T(8,128)(2,1)} %get-tuple-element.32.rows_a_ref, bf16[128,2048]{1,0:T(8,128)(2,1)} %get-tuple-element.33.rows_b_ref, f32[1,2048]{1,0:T(1,128)} %gain_ref.3, ...), custom_call_target="tpu_custom_call" | custom-call | flops 8405385216 | bytes 8208384 | tf_op jit(solution)/shard_map/logits/pallas_call | solution.py:315
  53.6 16.1 %logits.3 = (bf16[8016,256]{1,0:T(8,128)(2,1)}, bf16[8016,256]{1,0:T(8,128)(2,1)}, bf16[512,2048]{1,0:T(8,128)(2,1)}, f32[8,512]{1,0:T(8,128)}, f32[8,512]{1,0:T(8,128)}) custom-call(bf16[128,2048]{1,0:T(8,128)(2,1)} %collective-permute-done.4.rows_a_ref, bf16[128,2048]{1,0:T(8,128)(2,1)} %collective-permute-done.5.rows_b_ref, ...), custom_call_target="tpu_custom_call", output_to_operand_aliasing={{2}: (5, {})} | custom-call | flops 8405385216 | bytes 8208384 | tf_op jit(solution)/shard_map/logits/pallas_call | solution.py:315
  70.2 1.5 collective-permute-start.8
  76.3 1.5 totals.2.table_ref
  77.9 2.6 %collective-permute-start.11 = (f32[8,512]{1,0:T(8,128)}, f32[8,512]{1,0:T(8,128)}, u32[]{:S(2)}, u32[]{:S(2)}) collective-permute-start(f32[8,512]{1,0:T(8,128)} %totals.2.table_ref), channel_id=1, source_target_pairs={{0,12},{1,13},{2,14},{3,15},{4,8},{5,9},{6,10},{7,11},{8,4},{9,5},... | collective-permute-start | bytes 49160 | tf_op jit(solution)/shard_map/ppermute | solution.py:594
  83.7 1.7 %collective-permute-done.10.refs_1_ = f32[8,512]{1,0:T(8,128)} collective-permute-done((f32[8,512]{1,0:T(8,128)}, f32[8,512]{1,0:T(8,128)}, u32[]{:S(2)}, u32[]{:S(2)}) %collective-permute-start.10) | collective-permute-done | bytes 16416 | tf_op jit(solution)/shard_map/ppermute | solution.py:594
  85.4 1.6 totals.3.own_ref
  88.5 16.0 %dlogits.2 = (bf16[8016,512]{1,0:T(8,128)(2,1)}, bf16[128,2176]{1,0:T(8,128)(2,1)}, bf16[128,2176]{1,0:T(8,128)(2,1)}) custom-call(f32[16,512]{1,0:T(8,128)} %totals.3.own_ref, f32[16,512]{1,0:T(8,128)} %collective-permute-done.12.other_ref, s32[1,512]{1,0:T(1,128)} %sub.23.refs_0_.labels_ref, bf16[8016,256]{1,0:T(8,128)(2,1)} %get-tuple-element.41.ps_ref, ...), custom_call_target="tpu_custom_call" | custom-call | flops 8405385216 | bytes 16416768 | tf_op jit(solution)/shard_map/dlogits/pallas_call | solution.py:479
  104.6 1.5 collective-permute-start.15
  106.1 1.5 collective-permute-start.16
  107.6 16.2 %dlogits.3 = (bf16[8016,512]{1,0:T(8,128)(2,1)}, f32[128,2176]{1,0:T(8,128)}, f32[128,2176]{1,0:T(8,128)}) custom-call(f32[16,512]{1,0:T(8,128)} %totals.3.own_ref, f32[16,512]{1,0:T(8,128)} %collective-permute-done.12.other_ref, s32[1,512]{1,0:T(1,128)} %sub.23.refs_0_.labels_ref, ...), custom_call_target="tpu_custom_call", output_to_operand_aliasing={{0}: (7, {})} | custom-call | flops 8405385216 | bytes 16416768 | tf_op jit(solution)/shard_map/dlogits/pallas_call | solution.py:479
  126.4 1.7 %fold.3 = (f32[2,64,2176]{2,1,0:T(8,128)S(1)}, bf16[64,2176]{1,0:T(8,128)(2,1)S(1)}, bf16[64,2176]{1,0:T(8,128)(2,1)S(1)}) custom-call(f32[128,2176]{1,0:T(8,128)S(1)} %copy-done.1, f32[128,2176]{1,0:T(8,128)S(1)} %copy-done.2, bf16[128,2176]{1,0:T(8,128)(2,1)} %collective-permute-done.15.refs_2_, bf16[128,2176]{1,0:T(8,128)(2,1)} %collective-permute-done.16.refs_3_), custom_call_target="tpu_custom_call" | custom-call | flops 4096 | bytes 4096 | tf_op jit(solution)/shard_map/fold/pallas_call | solution.py:544
  129.2 10.3 %head_grad.3.refs_3_.refs_1_ = bf16[8016,2048]{1,0:T(8,128)(2,1)} custom-call(bf16[512,2048]{1,0:T(8,128)(2,1)S(1)} %copy-done, bf16[8016,512]{1,0:T(8,128)(2,1)} %get-tuple-element.52.d_ref, bf16[64,2176]{1,0:T(8,128)(2,1)S(1)} %get-tuple-element.49.refs_0_, bf16[64,2176]{1,0:T(8,128)(2,1)S(1)} %get-tuple-element.50.refs_1_), custom_call_target="tpu_custom_call" | custom-call | flops 6442450944 | bytes 15728640 | tf_op jit(solution)/shard_map/head_grad/pallas_call | solution.py:575
  140.7 7.9 %head_grad.4.refs_2_.refs_1_ = bf16[8016,2048]{1,0:T(8,128)(2,1)} custom-call(bf16[512,2048]{1,0:T(8,128)(2,1)S(1)} %copy-done, bf16[8016,512]{1,0:T(8,128)(2,1)} %get-tuple-element.52.d_ref, bf16[2,32,2176]{2,1,0:T(8,128)(2,1)S(1)} %get-tuple-element.54.refs_0_, bf16[8016,2048]{1,0:T(8,128)(2,1)} %head_grad.3.refs_3_.refs_1_), custom_call_target="tpu_custom_call", output_to_operand_aliasing={{}: (3, {})} | custom-call | flops 4294967296 | bytes 10485760 | tf_op jit(solution)/shard_map/head_grad/pallas_call | solution.py:575
  150.1 10.1 %head_grad.5 = bf16[8016,2048]{1,0:T(8,128)(2,1)} custom-call(bf16[512,2048]{1,0:T(8,128)(2,1)S(1)} %copy-done, bf16[8016,512]{1,0:T(8,128)(2,1)} %get-tuple-element.52.d_ref, bf16[2,16,2176]{2,1,0:T(8,128)(2,1)S(1)} %get-tuple-element.56.refs_0_, bf16[8016,2048]{1,0:T(8,128)(2,1)} %head_grad.4.refs_2_.refs_1_), custom_call_target="tpu_custom_call", output_to_operand_aliasing={{}: (3, {})} | custom-call | flops 6442450944 | bytes 15728640 | tf_op jit(solution)/shard_map/head_grad/pallas_call | solution.py:575
  (62 shorter events, 26.1 us)
Async XLA Ops:
  0.6 12.6 %collective-permute-start = (bf16[32,2048]{1,0:T(8,128)(2,1)}, bf16[32,2048]{1,0:T(8,128)(2,1)}, u32[]{:S(2)}, u32[]{:S(2)}) collective-permute-start(bf16[32,2048]{1,0:T(8,128)(2,1)} %bitcast.22), channel_id=1, source_target_pairs={{0,8},{1,9},{2,10},{3,11},{4,12},{5,13},{6,14},{7,15},{8,0},{9,1},... | collective-permute-start | bytes 393224 | tf_op jit(solution)/shard_map/ppermute | solution.py:594
  14.9 8.1 %collective-permute-start.1 = (bf16[64,2048]{1,0:T(8,128)(2,1)}, bf16[64,2048]{1,0:T(8,128)(2,1)}, u32[]{:S(2)}, u32[]{:S(2)}) collective-permute-start(bf16[64,2048]{1,0:T(8,128)(2,1)} %join.2.refs_0_), channel_id=1, source_target_pairs={{0,4},{1,5},{2,6},{3,7},{4,0},{5,1},{6,2},{7,3},{8,12},{9,13},{10,... | collective-permute-start | bytes 786440 | tf_op jit(solution)/shard_map/ppermute | solution.py:594
  24.9 7.2 %collective-permute-start.2 = (bf16[64,2048]{1,0:T(8,128)(2,1)}, bf16[64,2048]{1,0:T(8,128)(2,1)}, u32[]{:S(2)}, u32[]{:S(2)}) collective-permute-start(bf16[64,2048]{1,0:T(8,128)(2,1)} %get-tuple-element.30.low_a), channel_id=1, source_target_pairs={{0,2},{1,3},{2,0},{3,1},{4,6},{5,7},{6,4},{7,5},{8,10},{9,11},{10,... | collective-permute-start | bytes 786440 | tf_op jit(solution)/shard_map/ppermute | solution.py:594
  26.4 6.9 %collective-permute-start.3 = (bf16[64,2048]{1,0:T(8,128)(2,1)}, bf16[64,2048]{1,0:T(8,128)(2,1)}, u32[]{:S(2)}, u32[]{:S(2)}) collective-permute-start(bf16[64,2048]{1,0:T(8,128)(2,1)} %get-tuple-element.31.low_b), channel_id=1, source_target_pairs={{0,1},{1,0},{2,3},{3,2},{4,5},{5,4},{6,7},{7,6},{8,9},{9,8},{10,11... | collective-permute-start | bytes 786440 | tf_op jit(solution)/shard_map/ppermute | solution.py:594
  35.5 18.0 %collective-permute-start.4 = (bf16[128,2048]{1,0:T(8,128)(2,1)}, bf16[128,2048]{1,0:T(8,128)(2,1)}, u32[]{:S(2)}, u32[]{:S(2)}) collective-permute-start(bf16[128,2048]{1,0:T(8,128)(2,1)} %get-tuple-element.32.rows_a_ref), channel_id=1, source_target_pairs={{0,1},{1,0},{2,3},{3,2},{4,5},{5,4},{6,7},{7,6},{8,9},{9,8},{10,11... | collective-permute-start | bytes 1572872 | tf_op jit(solution)/shard_map/ppermute | solution.py:594
  37.0 16.6 %collective-permute-start.5 = (bf16[128,2048]{1,0:T(8,128)(2,1)}, bf16[128,2048]{1,0:T(8,128)(2,1)}, u32[]{:S(2)}, u32[]{:S(2)}) collective-permute-start(bf16[128,2048]{1,0:T(8,128)(2,1)} %get-tuple-element.33.rows_b_ref), channel_id=1, source_target_pairs={{0,2},{1,3},{2,0},{3,1},{4,6},{5,7},{6,4},{7,5},{8,10},{9,11},{10,... | collective-permute-start | bytes 1572872 | tf_op jit(solution)/shard_map/ppermute | solution.py:594
  69.7 18.9 %collective-permute-start.14 = (bf16[8016,256]{1,0:T(8,128)(2,1)}, bf16[8016,256]{1,0:T(8,128)(2,1)}, u32[]{:S(2)}, u32[]{:S(2)}) collective-permute-start(bf16[8016,256]{1,0:T(8,128)(2,1)} %get-tuple-element.41.ps_ref), channel_id=1, source_target_pairs={{0,16},{16,0},{1,17},{17,1},{2,18},{18,2},{3,19},{19,3},{4,20},{20... | collective-permute-start | bytes 12312584 | tf_op jit(solution)/shard_map/ppermute | solution.py:598
  69.7 37.8 %collective-permute-start.13 = (bf16[8016,256]{1,0:T(8,128)(2,1)}, bf16[8016,256]{1,0:T(8,128)(2,1)}, u32[]{:S(2)}, u32[]{:S(2)}) collective-permute-start(bf16[8016,256]{1,0:T(8,128)(2,1)} %get-tuple-element.39.ps_ref), channel_id=1, source_target_pairs={{0,16},{16,0},{1,17},{17,1},{2,18},{18,2},{3,19},{19,3},{4,20},{20... | collective-permute-start | bytes 12312584 | tf_op jit(solution)/shard_map/ppermute | solution.py:598
  70.2 5.0 %collective-permute-start.8 = (f32[8,512]{1,0:T(8,128)}, f32[8,512]{1,0:T(8,128)}, u32[]{:S(2)}, u32[]{:S(2)}) collective-permute-start(f32[8,512]{1,0:T(8,128)} %get-tuple-element.37.table_ref), channel_id=1, source_target_pairs={{0,3},{1,2},{2,1},{3,0},{4,7},{5,6},{6,5},{7,4},{8,11},{9,10},{10,... | collective-permute-start | bytes 49160 | tf_op jit(solution)/shard_map/ppermute | solution.py:594
  71.8 4.1 %collective-permute-start.7 = (f32[8,512]{1,0:T(8,128)}, f32[8,512]{1,0:T(8,128)}, u32[]{:S(2)}, u32[]{:S(2)}) collective-permute-start(f32[8,512]{1,0:T(8,128)} %get-tuple-element.37.table_ref), channel_id=1, source_target_pairs={{0,2},{1,3},{2,0},{3,1},{4,6},{5,7},{6,4},{7,5},{8,10},{9,11},{10,... | collective-permute-start | bytes 49160 | tf_op jit(solution)/shard_map/ppermute | solution.py:594
  72.3 4.1 %collective-permute-start.6 = (f32[8,512]{1,0:T(8,128)}, f32[8,512]{1,0:T(8,128)}, u32[]{:S(2)}, u32[]{:S(2)}) collective-permute-start(f32[8,512]{1,0:T(8,128)} %get-tuple-element.37.table_ref), channel_id=1, source_target_pairs={{0,1},{1,0},{2,3},{3,2},{4,5},{5,4},{6,7},{7,6},{8,9},{9,8},{10,11... | collective-permute-start | bytes 49160 | tf_op jit(solution)/shard_map/ppermute | solution.py:594
  77.9 5.9 %collective-permute-start.11 = (f32[8,512]{1,0:T(8,128)}, f32[8,512]{1,0:T(8,128)}, u32[]{:S(2)}, u32[]{:S(2)}) collective-permute-start(f32[8,512]{1,0:T(8,128)} %totals.2.table_ref), channel_id=1, source_target_pairs={{0,12},{1,13},{2,14},{3,15},{4,8},{5,9},{6,10},{7,11},{8,4},{9,5},... | collective-permute-start | bytes 49160 | tf_op jit(solution)/shard_map/ppermute | solution.py:594
  80.5 5.0 %collective-permute-start.10 = (f32[8,512]{1,0:T(8,128)}, f32[8,512]{1,0:T(8,128)}, u32[]{:S(2)}, u32[]{:S(2)}) collective-permute-start(f32[8,512]{1,0:T(8,128)} %totals.2.table_ref), channel_id=1, source_target_pairs={{0,8},{1,9},{2,10},{3,11},{4,12},{5,13},{6,14},{7,15},{8,0},{9,1},... | collective-permute-start | bytes 49160 | tf_op jit(solution)/shard_map/ppermute | solution.py:594
  80.9 4.5 %collective-permute-start.9 = (f32[8,512]{1,0:T(8,128)}, f32[8,512]{1,0:T(8,128)}, u32[]{:S(2)}, u32[]{:S(2)}) collective-permute-start(f32[8,512]{1,0:T(8,128)} %totals.2.table_ref), channel_id=1, source_target_pairs={{0,4},{1,5},{2,6},{3,7},{4,0},{5,1},{6,2},{7,3},{8,12},{9,13},{10,... | collective-permute-start | bytes 49160 | tf_op jit(solution)/shard_map/ppermute | solution.py:594
  87.0 1.6 collective-permute-start.12
  104.6 19.2 %collective-permute-start.15 = (bf16[128,2176]{1,0:T(8,128)(2,1)}, bf16[128,2176]{1,0:T(8,128)(2,1)}, u32[]{:S(2)}, u32[]{:S(2)}) collective-permute-start(bf16[128,2176]{1,0:T(8,128)(2,1)} %get-tuple-element.46), channel_id=1, source_target_pairs={{0,1},{1,0},{2,3},{3,2},{4,5},{5,4},{6,7},{7,6},{8,9},{9,8},{10,11... | collective-permute-start | bytes 1671176 | tf_op jit(solution)/shard_map/ppermute | solution.py:594
  106.1 17.7 %collective-permute-start.16 = (bf16[128,2176]{1,0:T(8,128)(2,1)}, bf16[128,2176]{1,0:T(8,128)(2,1)}, u32[]{:S(2)}, u32[]{:S(2)}) collective-permute-start(bf16[128,2176]{1,0:T(8,128)(2,1)} %get-tuple-element.47), channel_id=1, source_target_pairs={{0,2},{1,3},{2,0},{3,1},{4,6},{5,7},{6,4},{7,5},{8,10},{9,11},{10,... | collective-permute-start | bytes 1671176 | tf_op jit(solution)/shard_map/ppermute | solution.py:594
  128.1 11.4 %collective-permute-start.17 = (bf16[64,2176]{1,0:T(8,128)(2,1)S(1)}, bf16[64,2176]{1,0:T(8,128)(2,1)S(1)}, u32[]{:S(2)}, u32[]{:S(2)}) collective-permute-start(bf16[64,2176]{1,0:T(8,128)(2,1)S(1)} %get-tuple-element.49.refs_0_), channel_id=1, source_target_pairs={{0,2},{1,3},{2,0},{3,1},{4,6},{5,7},{6,4},{7,5},{8,10},{9,11},{10,... | collective-permute-start | bytes 835592 | tf_op jit(solution)/shard_map/ppermute | solution.py:594
  128.7 10.8 %collective-permute-start.18 = (bf16[64,2176]{1,0:T(8,128)(2,1)S(1)}, bf16[64,2176]{1,0:T(8,128)(2,1)S(1)}, u32[]{:S(2)}, u32[]{:S(2)}) collective-permute-start(bf16[64,2176]{1,0:T(8,128)(2,1)S(1)} %get-tuple-element.50.refs_1_), channel_id=1, source_target_pairs={{0,1},{1,0},{2,3},{3,2},{4,5},{5,4},{6,7},{7,6},{8,9},{9,8},{10,11... | collective-permute-start | bytes 835592 | tf_op jit(solution)/shard_map/ppermute | solution.py:594
  139.8 8.9 %collective-permute-start.19 = (bf16[2,32,2176]{2,1,0:T(8,128)(2,1)S(1)}, bf16[2,32,2176]{2,1,0:T(8,128)(2,1)S(1)}, u32[]{:S(2)}, u32[]{:S(2)}) collective-permute-start(bf16[2,32,2176]{2,1,0:T(8,128)(2,1)S(1)} %get-tuple-element.54.refs_0_), channel_id=1, source_target_pairs={{0,4},{1,5},{2,6},{3,7},{4,0},{5,1},{6,2},{7,3},{8,12},{9,13},{10,... | collective-permute-start | bytes 835592 | tf_op jit(solution)/shard_map/ppermute | solution.py:594
  148.8 11.6 %copy-start.4 = (f32[1,2048]{1,0:T(1,128)S(1)}, f32[1,2048]{1,0:T(1,128)}, u32[]{:S(2)}) copy-start(f32[1,2048]{1,0:T(1,128)} %gain_ref.3) | copy-start | bytes 24580
  148.8 12.5 %copy-start.5 = (f32[1,16]{1,0:T(1,128)S(1)}, f32[1,16]{1,0:T(1,128)}, u32[]{:S(2)}) copy-start(f32[1,16]{1,0:T(1,128)} %get-tuple-element.61) | copy-start | bytes 196
  148.8 12.5 %copy-start.6 = (f32[1,16]{1,0:T(1,128)S(1)}, f32[1,16]{1,0:T(1,128)}, u32[]{:S(2)}) copy-start(f32[1,16]{1,0:T(1,128)} %get-tuple-element.62) | copy-start | bytes 196
  148.8 11.3 %collective-permute-start.20 = (bf16[2,16,2176]{2,1,0:T(8,128)(2,1)S(1)}, bf16[2,16,2176]{2,1,0:T(8,128)(2,1)S(1)}, u32[]{:S(2)}, u32[]{:S(2)}) collective-permute-start(bf16[2,16,2176]{2,1,0:T(8,128)(2,1)S(1)} %get-tuple-element.56.refs_0_), channel_id=1, source_target_pairs={{0,8},{1,9},{2,10},{3,11},{4,12},{5,13},{6,14},{7,15},{8,0},{9,1},... | collective-permute-start | bytes 417800 | tf_op jit(solution)/shard_map/ppermute | solution.py:594
  (4 other events, 19.7 us)

commit v4 on v3

--- a/solution.py
+++ b/solution.py
@@ -553,6 +553,33 @@
     )(*operands)
 
 
+def finish_kernel(keep_ref, got_ref, rows_ref, gain_ref, base_ref, grad_ref, loss_ref):
+    width = rows_ref.shape[1]
+    half = keep_ref.shape[1]
+    for part in range(2):
+        here = slice(part * half, (part + 1) * half)
+        total = keep_ref[part] + got_ref[part].astype(jnp.float32)
+        values = rows_ref[here, :].astype(jnp.float32)
+        inverse = lax.rsqrt(jnp.mean(values * values, axis=-1, keepdims=True) + EPS)
+        scaled = gain_ref[...] * total[:, :width]
+        inner = jnp.mean(scaled * values, axis=-1, keepdims=True)
+        grad_ref[here, :] = (inverse * scaled - values * inverse**3 * inner).astype(grad_ref.dtype)
+        cross = total[:, width : width + 1] + total[:, width + 1 : width + 2]
+        loss_ref[:, here] = base_ref[:, here] + BETA * jnp.broadcast_to(cross, (half, LANES)).T[0:1, :]
+
+
+def run_finish(keep, got, rows, gain, base):
+    return pl.pallas_call(
+        finish_kernel,
+        in_specs=[whole_vmem()] * 5,
+        out_specs=[whole_vmem()] * 2,
+        out_shape=[jax.ShapeDtypeStruct(rows.shape, rows.dtype), jax.ShapeDtypeStruct(base.shape, jnp.float32)],
+        compiler_params=pltpu.CompilerParams(vmem_limit_bytes=VMEM_SHARED),
+        cost_estimate=SMALL,
+        name="finish",
+    )(keep, got, rows, gain, base)
+
+
 def head_grad_kernel(normed_ref, d_ref, *refs):
     out_ref = refs[-1]
     out_ref[...] = jnp.dot(d_ref[...], normed_ref[...], preferred_element_type=jnp.float32).astype(out_ref.dtype)
@@ -691,6 +718,8 @@
             got = [moved(send[0], 2), moved(send[1], 1)]
         else:
             got = [moved(send[0], 1 << step)]
+        if step == bits - 1 and half % 16 == 0:
+            break
         cut = keep.shape[1] // 2
         if step < bits - 1 and cut % 16 == 0:
             summed = run_fold((keep,), got, 1, grad)
@@ -700,13 +729,17 @@
                 summed = [total[:, :cut], pack(total[:, cut:], width)]
             else:
                 summed = total
+    quarter = tokens // 4
+    own = lambda row: jnp.concatenate([row[:half], row[quarter : quarter + half]])
+    base = own(table[0]) - own(table[1])
+    if half % 16 == 0:
+        hidden_grad, token_loss = run_finish(keep, got[0], own_rows, gain_row[None], base[None])
+        return (token_loss, grad.T[None], hidden_grad[None])
     summed = summed.reshape(tok_dev, -1)
     cross = summed[:, width] + summed[:, width + 1]
     summed = summed[:, :width]
 
-    quarter = tokens // 4
-    own = lambda row: jnp.concatenate([row[:half], row[quarter : quarter + half]])
-    token_loss = own(table[0]) - own(table[1]) + BETA * cross
+    token_loss = base + BETA * cross
     values = own_rows.astype(jnp.float32)
     inverse = lax.rsqrt(jnp.mean(values * values, axis=-1, keepdims=True) + EPS)
     scaled = gain_row * summed

time: 163 us -> 162 us (level)
  other arithmetic: 2.45 us -> 0.77 us
  transfers between devices with their start and end apart: 21 -> 21, of which waited for: 9 -> 9; matrix products, arithmetic and copies ran while one was open for 2% -> 2% of each run, Pallas kernels for 56% -> 57%
where the time goes in v4:
time: 162 us; the launch traced here: 161 us
  Pallas kernels  116 us (72%)
  starting transfers between devices  25.4 us (16%)
  waiting for transfers between devices  12.6 us (8%)
  local copies, waits for them, and re-layouts  5.41 us (3%)
    pallas_call x2, Pallas kernels, run_dlogits(): pl.pallas_call(functools.partial(dlogits_kernel, tile, tiles, group), gri...  32.2 us
    pallas_call x2, Pallas kernels, run_logits(): pl.pallas_call(functools.partial(logits_kernel, tile, tiles, group), grid...  32.2 us
    pallas_call x3, Pallas kernels, run_head_grad(): pl.pallas_call(head_grad_kernel, grid=(count,), in_specs=in_specs, out_sp...  28.3 us
    ppermute x18, starting transfers between devices, moved(): return lax.ppermute(value, 'fsdp', [(i, i ^ offset) for i in range(n)])  24.8 us
    ppermute x18, waiting for transfers between devices, moved(): return lax.ppermute(value, 'fsdp', [(i, i ^ offset) for i in range(n)])  11.9 us
    pallas_call x2, Pallas kernels, run_load(): pl.pallas_call(functools.partial(load_kernel, first, rows), in_specs=in_s...  11.6 us
    pallas_call x2, Pallas kernels, run_join(): pl.pallas_call(functools.partial(join_kernel, len(pieces), split), in_spe...  3.53 us
  transfers between devices with their start and end apart: 21, of which 9 were waited for; matrix products, arithmetic and copies ran while one was open for 2% of the time, Pallas kernels for 57%

profile of v4, /device:TPU:0, one launch (start us, length us, event | category | flops | bytes accessed | tf_op | source)
XLA Modules:
  0.0 161.1 jit_solution(12715763777279084913)
XLA Ops:
  0.6 4.1 %collective-permute-start = (bf16[32,2048]{1,0:T(8,128)(2,1)}, bf16[32,2048]{1,0:T(8,128)(2,1)}, u32[]{:S(2)}, u32[]{:S(2)}) collective-permute-start(bf16[32,2048]{1,0:T(8,128)(2,1)} %bitcast.8), channel_id=1, source_target_pairs={{0,8},{1,9},{2,10},{3,11},{4,12},{5,13},{6,14},{7,15},{8,0},{9,1},... | collective-permute-start | bytes 393224 | tf_op jit(solution)/shard_map/ppermute | solution.py:621
  7.4 5.8 %load.2.refs_2_.refs_1_ = bf16[8016,2048]{1,0:T(8,128)(2,1)S(1)} custom-call(bf16[8016,2048]{1,0:T(8,128)(2,1)} %bitcast.12, s32[1,512]{1,0:T(1,128)} %sub.20.refs_0_.labels_ref), custom_call_target="tpu_custom_call" | custom-call | bytes 32899072 | tf_op jit(solution)/shard_map/load/pallas_call | solution.py:85
  13.2 1.7 %join.2.refs_0_ = bf16[64,2048]{1,0:T(8,128)(2,1)} custom-call(bf16[32,2048]{1,0:T(8,128)(2,1)} %bitcast.9, bf16[32,2048]{1,0:T(8,128)(2,1)} %collective-permute-done.refs_1_, bf16[8016,2048]{1,0:T(8,128)(2,1)S(1)} %load.2.refs_2_.refs_1_), custom_call_target="tpu_custom_call" | custom-call | flops 4096 | bytes 4096 | tf_op jit(solution)/shard_map/join/pallas_call | solution.py:115
  14.9 1.6 collective-permute-start.1
  16.5 5.8 %load.3.refs_2_.w_ref.refs_3_.refs_4_ = bf16[8016,2048]{1,0:T(8,128)(2,1)S(1)} custom-call(bf16[8016,2048]{1,0:T(8,128)(2,1)} %bitcast.13, bf16[64,2048]{1,0:T(8,128)(2,1)} %join.2.refs_0_, bf16[8016,2048]{1,0:T(8,128)(2,1)S(1)} %load.2.refs_2_.refs_1_), custom_call_target="tpu_custom_call", output_to_operand_aliasing={{}: (2, {})} | custom-call | bytes 32768000 | tf_op jit(solution)/shard_map/load/pallas_call | solution.py:85
  23.0 1.8 %join.3 = (bf16[64,2048]{1,0:T(8,128)(2,1)}, bf16[64,2048]{1,0:T(8,128)(2,1)}) custom-call(bf16[64,2048]{1,0:T(8,128)(2,1)} %join.2.refs_0_, bf16[64,2048]{1,0:T(8,128)(2,1)} %collective-permute-done.1.refs_1_, bf16[8016,2048]{1,0:T(8,128)(2,1)S(1)} %load.3.refs_2_.w_ref.refs_3_.refs_4_), custom_call_target="tpu_custom_call" | custom-call | flops 4096 | bytes 4096 | tf_op jit(solution)/shard_map/join/pallas_call | solution.py:115
  24.9 1.5 collective-permute-start.2
  27.9 4.2 %collective-permute-done.2.high_a = bf16[64,2048]{1,0:T(8,128)(2,1)} collective-permute-done((bf16[64,2048]{1,0:T(8,128)(2,1)}, bf16[64,2048]{1,0:T(8,128)(2,1)}, u32[]{:S(2)}, u32[]{:S(2)}) %collective-permute-start.2) | collective-permute-done | bytes 262176 | tf_op jit(solution)/shard_map/ppermute | solution.py:621
  33.3 2.2 %stack.1 = (bf16[128,2048]{1,0:T(8,128)(2,1)}, bf16[128,2048]{1,0:T(8,128)(2,1)}) custom-call(bf16[8016,2048]{1,0:T(8,128)(2,1)S(1)} %load.3.refs_2_.w_ref.refs_3_.refs_4_, bf16[64,2048]{1,0:T(8,128)(2,1)} %get-tuple-element.32.low_a, bf16[64,2048]{1,0:T(8,128)(2,1)} %collective-permute-done.2.high_a, bf16[64,2048]{1,0:T(8,128)(2,1)} %get-tuple-element.33.low_b, ...), custom_call_target="tpu_custom_call" | custom-call | flops 4096 | bytes 4096 | tf_op jit(solution)/shard_map/stack/pallas_call | solution.py:135
  37.5 16.1 %logits.2 = (bf16[8016,256]{1,0:T(8,128)(2,1)}, bf16[8016,256]{1,0:T(8,128)(2,1)}, bf16[512,2048]{1,0:T(8,128)(2,1)}, f32[8,256]{1,0:T(8,128)}, f32[8,256]{1,0:T(8,128)}) custom-call(bf16[128,2048]{1,0:T(8,128)(2,1)} %get-tuple-element.34.rows_a_ref, bf16[128,2048]{1,0:T(8,128)(2,1)} %get-tuple-element.35.rows_b_ref, f32[1,2048]{1,0:T(1,128)} %gain_ref.5, ...), custom_call_target="tpu_custom_call" | custom-call | flops 8405385216 | bytes 8208384 | tf_op jit(solution)/shard_map/logits/pallas_call | solution.py:315
  53.5 16.1 %logits.3 = (bf16[8016,256]{1,0:T(8,128)(2,1)}, bf16[8016,256]{1,0:T(8,128)(2,1)}, bf16[512,2048]{1,0:T(8,128)(2,1)}, f32[8,512]{1,0:T(8,128)}, f32[8,512]{1,0:T(8,128)}) custom-call(bf16[128,2048]{1,0:T(8,128)(2,1)} %collective-permute-done.4.rows_a_ref, bf16[128,2048]{1,0:T(8,128)(2,1)} %collective-permute-done.5.rows_b_ref, ...), custom_call_target="tpu_custom_call", output_to_operand_aliasing={{2}: (5, {})} | custom-call | flops 8405385216 | bytes 8208384 | tf_op jit(solution)/shard_map/logits/pallas_call | solution.py:315
  72.2 1.5 collective-permute-start.6
  76.3 1.5 totals.2.table_ref
  77.8 2.6 %collective-permute-start.11 = (f32[8,512]{1,0:T(8,128)}, f32[8,512]{1,0:T(8,128)}, u32[]{:S(2)}, u32[]{:S(2)}) collective-permute-start(f32[8,512]{1,0:T(8,128)} %totals.2.table_ref), channel_id=1, source_target_pairs={{0,12},{1,13},{2,14},{3,15},{4,8},{5,9},{6,10},{7,11},{8,4},{9,5},... | collective-permute-start | bytes 49160 | tf_op jit(solution)/shard_map/ppermute | solution.py:621
  83.7 1.7 %collective-permute-done.10.refs_1_ = f32[8,512]{1,0:T(8,128)} collective-permute-done((f32[8,512]{1,0:T(8,128)}, f32[8,512]{1,0:T(8,128)}, u32[]{:S(2)}, u32[]{:S(2)}) %collective-permute-start.10) | collective-permute-done | bytes 16416 | tf_op jit(solution)/shard_map/ppermute | solution.py:621
  85.4 1.6 totals.3.own_ref
  88.6 16.0 %dlogits.2 = (bf16[8016,512]{1,0:T(8,128)(2,1)}, bf16[128,2176]{1,0:T(8,128)(2,1)}, bf16[128,2176]{1,0:T(8,128)(2,1)}) custom-call(f32[16,512]{1,0:T(8,128)} %totals.3.own_ref, f32[16,512]{1,0:T(8,128)} %collective-permute-done.12.other_ref, s32[1,512]{1,0:T(1,128)} %sub.20.refs_0_.labels_ref, bf16[8016,256]{1,0:T(8,128)(2,1)} %get-tuple-element.43.ps_ref, ...), custom_call_target="tpu_custom_call" | custom-call | flops 8405385216 | bytes 16416768 | tf_op jit(solution)/shard_map/dlogits/pallas_call | solution.py:479
  104.6 1.5 collective-permute-start.15
  106.1 1.5 collective-permute-start.16
  107.6 16.2 %dlogits.3 = (bf16[8016,512]{1,0:T(8,128)(2,1)}, f32[128,2176]{1,0:T(8,128)}, f32[128,2176]{1,0:T(8,128)}) custom-call(f32[16,512]{1,0:T(8,128)} %totals.3.own_ref, f32[16,512]{1,0:T(8,128)} %collective-permute-done.12.other_ref, s32[1,512]{1,0:T(1,128)} %sub.20.refs_0_.labels_ref, ...), custom_call_target="tpu_custom_call", output_to_operand_aliasing={{0}: (7, {})} | custom-call | flops 8405385216 | bytes 16416768 | tf_op jit(solution)/shard_map/dlogits/pallas_call | solution.py:479
  126.4 1.7 %fold.3 = (f32[2,64,2176]{2,1,0:T(8,128)S(1)}, bf16[64,2176]{1,0:T(8,128)(2,1)S(1)}, bf16[64,2176]{1,0:T(8,128)(2,1)S(1)}) custom-call(f32[128,2176]{1,0:T(8,128)S(1)} %copy-done.1, f32[128,2176]{1,0:T(8,128)S(1)} %copy-done.2, bf16[128,2176]{1,0:T(8,128)(2,1)} %collective-permute-done.15.refs_2_, bf16[128,2176]{1,0:T(8,128)(2,1)} %collective-permute-done.16.refs_3_), custom_call_target="tpu_custom_call" | custom-call | flops 4096 | bytes 4096 | tf_op jit(solution)/shard_map/fold/pallas_call | solution.py:544
  129.3 10.3 %head_grad.3.refs_3_.refs_1_ = bf16[8016,2048]{1,0:T(8,128)(2,1)} custom-call(bf16[512,2048]{1,0:T(8,128)(2,1)S(1)} %copy-done, bf16[8016,512]{1,0:T(8,128)(2,1)} %get-tuple-element.54.d_ref, bf16[64,2176]{1,0:T(8,128)(2,1)S(1)} %get-tuple-element.51.refs_0_, bf16[64,2176]{1,0:T(8,128)(2,1)S(1)} %get-tuple-element.52.refs_1_), custom_call_target="tpu_custom_call" | custom-call | flops 6442450944 | bytes 15728640 | tf_op jit(solution)/shard_map/head_grad/pallas_call | solution.py:602
  140.7 7.9 %head_grad.4.refs_2_.refs_1_ = bf16[8016,2048]{1,0:T(8,128)(2,1)} custom-call(bf16[512,2048]{1,0:T(8,128)(2,1)S(1)} %copy-done, bf16[8016,512]{1,0:T(8,128)(2,1)} %get-tuple-element.54.d_ref, bf16[2,32,2176]{2,1,0:T(8,128)(2,1)S(1)} %get-tuple-element.56.refs_0_, bf16[8016,2048]{1,0:T(8,128)(2,1)} %head_grad.3.refs_3_.refs_1_), custom_call_target="tpu_custom_call", output_to_operand_aliasing={{}: (3, {})} | custom-call | flops 4294967296 | bytes 10485760 | tf_op jit(solution)/shard_map/head_grad/pallas_call | solution.py:602
  150.1 10.1 %head_grad.5 = bf16[8016,2048]{1,0:T(8,128)(2,1)} custom-call(bf16[512,2048]{1,0:T(8,128)(2,1)S(1)} %copy-done, bf16[8016,512]{1,0:T(8,128)(2,1)} %get-tuple-element.54.d_ref, bf16[2,16,2176]{2,1,0:T(8,128)(2,1)S(1)} %get-tuple-element.58.refs_0_, bf16[8016,2048]{1,0:T(8,128)(2,1)} %head_grad.4.refs_2_.refs_1_), custom_call_target="tpu_custom_call", output_to_operand_aliasing={{}: (3, {})} | custom-call | flops 6442450944 | bytes 15728640 | tf_op jit(solution)/shard_map/head_grad/pallas_call | solution.py:602
  (54 shorter events, 25.2 us)
Async XLA Ops:
  0.6 12.6 %collective-permute-start = (bf16[32,2048]{1,0:T(8,128)(2,1)}, bf16[32,2048]{1,0:T(8,128)(2,1)}, u32[]{:S(2)}, u32[]{:S(2)}) collective-permute-start(bf16[32,2048]{1,0:T(8,128)(2,1)} %bitcast.8), channel_id=1, source_target_pairs={{0,8},{1,9},{2,10},{3,11},{4,12},{5,13},{6,14},{7,15},{8,0},{9,1},... | collective-permute-start | bytes 393224 | tf_op jit(solution)/shard_map/ppermute | solution.py:621
  14.9 8.1 %collective-permute-start.1 = (bf16[64,2048]{1,0:T(8,128)(2,1)}, bf16[64,2048]{1,0:T(8,128)(2,1)}, u32[]{:S(2)}, u32[]{:S(2)}) collective-permute-start(bf16[64,2048]{1,0:T(8,128)(2,1)} %join.2.refs_0_), channel_id=1, source_target_pairs={{0,4},{1,5},{2,6},{3,7},{4,0},{5,1},{6,2},{7,3},{8,12},{9,13},{10,... | collective-permute-start | bytes 786440 | tf_op jit(solution)/shard_map/ppermute | solution.py:621
  24.9 7.2 %collective-permute-start.2 = (bf16[64,2048]{1,0:T(8,128)(2,1)}, bf16[64,2048]{1,0:T(8,128)(2,1)}, u32[]{:S(2)}, u32[]{:S(2)}) collective-permute-start(bf16[64,2048]{1,0:T(8,128)(2,1)} %get-tuple-element.32.low_a), channel_id=1, source_target_pairs={{0,2},{1,3},{2,0},{3,1},{4,6},{5,7},{6,4},{7,5},{8,10},{9,11},{10,... | collective-permute-start | bytes 786440 | tf_op jit(solution)/shard_map/ppermute | solution.py:621
  26.4 6.9 %collective-permute-start.3 = (bf16[64,2048]{1,0:T(8,128)(2,1)}, bf16[64,2048]{1,0:T(8,128)(2,1)}, u32[]{:S(2)}, u32[]{:S(2)}) collective-permute-start(bf16[64,2048]{1,0:T(8,128)(2,1)} %get-tuple-element.33.low_b), channel_id=1, source_target_pairs={{0,1},{1,0},{2,3},{3,2},{4,5},{5,4},{6,7},{7,6},{8,9},{9,8},{10,11... | collective-permute-start | bytes 786440 | tf_op jit(solution)/shard_map/ppermute | solution.py:621
  35.5 18.1 %collective-permute-start.4 = (bf16[128,2048]{1,0:T(8,128)(2,1)}, bf16[128,2048]{1,0:T(8,128)(2,1)}, u32[]{:S(2)}, u32[]{:S(2)}) collective-permute-start(bf16[128,2048]{1,0:T(8,128)(2,1)} %get-tuple-element.34.rows_a_ref), channel_id=1, source_target_pairs={{0,1},{1,0},{2,3},{3,2},{4,5},{5,4},{6,7},{7,6},{8,9},{9,8},{10,11... | collective-permute-start | bytes 1572872 | tf_op jit(solution)/shard_map/ppermute | solution.py:621
  37.0 16.6 %collective-permute-start.5 = (bf16[128,2048]{1,0:T(8,128)(2,1)}, bf16[128,2048]{1,0:T(8,128)(2,1)}, u32[]{:S(2)}, u32[]{:S(2)}) collective-permute-start(bf16[128,2048]{1,0:T(8,128)(2,1)} %get-tuple-element.35.rows_b_ref), channel_id=1, source_target_pairs={{0,2},{1,3},{2,0},{3,1},{4,6},{5,7},{6,4},{7,5},{8,10},{9,11},{10,... | collective-permute-start | bytes 1572872 | tf_op jit(solution)/shard_map/ppermute | solution.py:621
  69.7 18.9 %collective-permute-start.14 = (bf16[8016,256]{1,0:T(8,128)(2,1)}, bf16[8016,256]{1,0:T(8,128)(2,1)}, u32[]{:S(2)}, u32[]{:S(2)}) collective-permute-start(bf16[8016,256]{1,0:T(8,128)(2,1)} %get-tuple-element.43.ps_ref), channel_id=1, source_target_pairs={{0,16},{16,0},{1,17},{17,1},{2,18},{18,2},{3,19},{19,3},{4,20},{20... | collective-permute-start | bytes 12312584 | tf_op jit(solution)/shard_map/ppermute | solution.py:625
  69.8 37.9 %collective-permute-start.13 = (bf16[8016,256]{1,0:T(8,128)(2,1)}, bf16[8016,256]{1,0:T(8,128)(2,1)}, u32[]{:S(2)}, u32[]{:S(2)}) collective-permute-start(bf16[8016,256]{1,0:T(8,128)(2,1)} %get-tuple-element.41.ps_ref), channel_id=1, source_target_pairs={{0,16},{16,0},{1,17},{17,1},{2,18},{18,2},{3,19},{19,3},{4,20},{20... | collective-permute-start | bytes 12312584 | tf_op jit(solution)/shard_map/ppermute | solution.py:625
  70.3 5.0 %collective-permute-start.8 = (f32[8,512]{1,0:T(8,128)}, f32[8,512]{1,0:T(8,128)}, u32[]{:S(2)}, u32[]{:S(2)}) collective-permute-start(f32[8,512]{1,0:T(8,128)} %get-tuple-element.39.table_ref), channel_id=1, source_target_pairs={{0,3},{1,2},{2,1},{3,0},{4,7},{5,6},{6,5},{7,4},{8,11},{9,10},{10,... | collective-permute-start | bytes 49160 | tf_op jit(solution)/shard_map/ppermute | solution.py:621
  71.7 4.1 %collective-permute-start.7 = (f32[8,512]{1,0:T(8,128)}, f32[8,512]{1,0:T(8,128)}, u32[]{:S(2)}, u32[]{:S(2)}) collective-permute-start(f32[8,512]{1,0:T(8,128)} %get-tuple-element.39.table_ref), channel_id=1, source_target_pairs={{0,2},{1,3},{2,0},{3,1},{4,6},{5,7},{6,4},{7,5},{8,10},{9,11},{10,... | collective-permute-start | bytes 49160 | tf_op jit(solution)/shard_map/ppermute | solution.py:621
  72.2 4.1 %collective-permute-start.6 = (f32[8,512]{1,0:T(8,128)}, f32[8,512]{1,0:T(8,128)}, u32[]{:S(2)}, u32[]{:S(2)}) collective-permute-start(f32[8,512]{1,0:T(8,128)} %get-tuple-element.39.table_ref), channel_id=1, source_target_pairs={{0,1},{1,0},{2,3},{3,2},{4,5},{5,4},{6,7},{7,6},{8,9},{9,8},{10,11... | collective-permute-start | bytes 49160 | tf_op jit(solution)/shard_map/ppermute | solution.py:621
  77.8 5.9 %collective-permute-start.11 = (f32[8,512]{1,0:T(8,128)}, f32[8,512]{1,0:T(8,128)}, u32[]{:S(2)}, u32[]{:S(2)}) collective-permute-start(f32[8,512]{1,0:T(8,128)} %totals.2.table_ref), channel_id=1, source_target_pairs={{0,12},{1,13},{2,14},{3,15},{4,8},{5,9},{6,10},{7,11},{8,4},{9,5},... | collective-permute-start | bytes 49160 | tf_op jit(solution)/shard_map/ppermute | solution.py:621
  80.5 5.0 %collective-permute-start.10 = (f32[8,512]{1,0:T(8,128)}, f32[8,512]{1,0:T(8,128)}, u32[]{:S(2)}, u32[]{:S(2)}) collective-permute-start(f32[8,512]{1,0:T(8,128)} %totals.2.table_ref), channel_id=1, source_target_pairs={{0,8},{1,9},{2,10},{3,11},{4,12},{5,13},{6,14},{7,15},{8,0},{9,1},... | collective-permute-start | bytes 49160 | tf_op jit(solution)/shard_map/ppermute | solution.py:621
  80.9 4.5 %collective-permute-start.9 = (f32[8,512]{1,0:T(8,128)}, f32[8,512]{1,0:T(8,128)}, u32[]{:S(2)}, u32[]{:S(2)}) collective-permute-start(f32[8,512]{1,0:T(8,128)} %totals.2.table_ref), channel_id=1, source_target_pairs={{0,4},{1,5},{2,6},{3,7},{4,0},{5,1},{6,2},{7,3},{8,12},{9,13},{10,... | collective-permute-start | bytes 49160 | tf_op jit(solution)/shard_map/ppermute | solution.py:621
  87.0 1.6 collective-permute-start.12
  104.6 19.2 %collective-permute-start.15 = (bf16[128,2176]{1,0:T(8,128)(2,1)}, bf16[128,2176]{1,0:T(8,128)(2,1)}, u32[]{:S(2)}, u32[]{:S(2)}) collective-permute-start(bf16[128,2176]{1,0:T(8,128)(2,1)} %get-tuple-element.48), channel_id=1, source_target_pairs={{0,1},{1,0},{2,3},{3,2},{4,5},{5,4},{6,7},{7,6},{8,9},{9,8},{10,11... | collective-permute-start | bytes 1671176 | tf_op jit(solution)/shard_map/ppermute | solution.py:621
  106.1 17.7 %collective-permute-start.16 = (bf16[128,2176]{1,0:T(8,128)(2,1)}, bf16[128,2176]{1,0:T(8,128)(2,1)}, u32[]{:S(2)}, u32[]{:S(2)}) collective-permute-start(bf16[128,2176]{1,0:T(8,128)(2,1)} %get-tuple-element.49), channel_id=1, source_target_pairs={{0,2},{1,3},{2,0},{3,1},{4,6},{5,7},{6,4},{7,5},{8,10},{9,11},{10,... | collective-permute-start | bytes 1671176 | tf_op jit(solution)/shard_map/ppermute | solution.py:621
  123.8 5.5 %copy-start = (bf16[512,2048]{1,0:T(8,128)(2,1)S(1)}, bf16[512,2048]{1,0:T(8,128)(2,1)}, u32[]{:S(2)}) copy-start(bf16[512,2048]{1,0:T(8,128)(2,1)} %get-tuple-element.53.normed_ref) | copy-start | bytes 6291460
  128.2 11.4 %collective-permute-start.17 = (bf16[64,2176]{1,0:T(8,128)(2,1)S(1)}, bf16[64,2176]{1,0:T(8,128)(2,1)S(1)}, u32[]{:S(2)}, u32[]{:S(2)}) collective-permute-start(bf16[64,2176]{1,0:T(8,128)(2,1)S(1)} %get-tuple-element.51.refs_0_), channel_id=1, source_target_pairs={{0,2},{1,3},{2,0},{3,1},{4,6},{5,7},{6,4},{7,5},{8,10},{9,11},{10,... | collective-permute-start | bytes 835592 | tf_op jit(solution)/shard_map/ppermute | solution.py:621
  128.7 10.9 %collective-permute-start.18 = (bf16[64,2176]{1,0:T(8,128)(2,1)S(1)}, bf16[64,2176]{1,0:T(8,128)(2,1)S(1)}, u32[]{:S(2)}, u32[]{:S(2)}) collective-permute-start(bf16[64,2176]{1,0:T(8,128)(2,1)S(1)} %get-tuple-element.52.refs_1_), channel_id=1, source_target_pairs={{0,1},{1,0},{2,3},{3,2},{4,5},{5,4},{6,7},{7,6},{8,9},{9,8},{10,11... | collective-permute-start | bytes 835592 | tf_op jit(solution)/shard_map/ppermute | solution.py:621
  139.8 8.8 %collective-permute-start.19 = (bf16[2,32,2176]{2,1,0:T(8,128)(2,1)S(1)}, bf16[2,32,2176]{2,1,0:T(8,128)(2,1)S(1)}, u32[]{:S(2)}, u32[]{:S(2)}) collective-permute-start(bf16[2,32,2176]{2,1,0:T(8,128)(2,1)S(1)} %get-tuple-element.56.refs_0_), channel_id=1, source_target_pairs={{0,4},{1,5},{2,6},{3,7},{4,0},{5,1},{6,2},{7,3},{8,12},{9,13},{10,... | collective-permute-start | bytes 835592 | tf_op jit(solution)/shard_map/ppermute | solution.py:621
  148.8 11.3 %copy-start.3 = (bf16[1,32,2048]{2,1,0:T(8,128)(2,1)S(1)}, bf16[1,32,2048]{2,1,0:T(8,128)(2,1)}, u32[]{:S(2)}) copy-start(bf16[1,32,2048]{2,1,0:T(8,128)(2,1)} %param.6) | copy-start | bytes 393220
  148.8 11.3 %copy-start.4 = (f32[1,2048]{1,0:T(1,128)S(1)}, f32[1,2048]{1,0:T(1,128)}, u32[]{:S(2)}) copy-start(f32[1,2048]{1,0:T(1,128)} %gain_ref.5) | copy-start | bytes 24580
  148.8 11.3 %collective-permute-start.20 = (bf16[2,16,2176]{2,1,0:T(8,128)(2,1)S(1)}, bf16[2,16,2176]{2,1,0:T(8,128)(2,1)S(1)}, u32[]{:S(2)}, u32[]{:S(2)}) collective-permute-start(bf16[2,16,2176]{2,1,0:T(8,128)(2,1)S(1)} %get-tuple-element.58.refs_0_), channel_id=1, source_target_pairs={{0,8},{1,9},{2,10},{3,11},{4,12},{5,13},{6,14},{7,15},{8,0},{9,1},... | collective-permute-start | bytes 417800 | tf_op jit(solution)/shard_map/ppermute | solution.py:621
  (2 other events, 2.6 us)
